TPU v7x, 256 devices: a whole 4x4x8 slice. The times are simulated.
256 devices in a mesh: prow: 16 (over z, core), pcol: 16 (over x, y).
Axes of the slice: x: 4, y: 4, z: 8, core: 2. Of those that a mesh axis runs over, the one named last changes fastest.
Arguments:
- x_done: float32 [2, 512, 32768], P(None, None, 'prow'), may hold values from -6 to 6
- l_below: float32 [2, 2, 1024, 32768], P(None, None, 'pcol', 'prow'), may hold values from -0.0234375 to 0.0234375
- rhs_window: float32 [2, 512, 2, 1024], P(None, 'prow', None, 'pcol'), may hold values from -6 to 6
- inv_diag: float32 [2, 2, 1024, 1024], P(None, None, 'pcol'), may hold values from -0.5 to 2
- l_couple: float32 [2, 1024, 1024], P(None, 'pcol'), may hold values from -0.125 to 0.125
Outputs:
- x_window: float32 [2, 512, 2, 1024], P(None, 'prow', None, 'pcol')
All inputs are finite; a program needn't handle non-finite values.
Results may differ from a plain program's by a relative error of at most 0.00007.
Values sent between devices are 32-bit elements; how exact they have to be, the bound alone decides.
No kernel may reach another device: no remote copies, remote signals or barrier semaphores. Data moves between devices by JAX's collectives and lax.ppermute only.
A program may use at most 64 MiB of HBM per device.

v0:
```python
import jax
import jax.numpy as jnp
from jax import lax
from jax.experimental import pallas as pl
from jax.experimental.pallas import tpu as pltpu
from jax.sharding import PartitionSpec as P

BF = jnp.bfloat16
F32 = jnp.float32
CHUNKS = 4
VMEM_LIMIT = 16 * 1024 * 1024
UPDATE_VMEM = 53 * 1024 * 1024
VMEM = pl.BlockSpec(memory_space=pltpu.VMEM)


def split(mat):
    high = mat.astype(BF)
    return high, (mat - high.astype(F32)).astype(BF)


def dot_split(left, right):
    left_high, left_low = split(left)
    right_high, right_low = split(right)
    return lax.dot_general(
        jnp.concatenate([left_high, left_low, left_high], axis=1),
        jnp.concatenate([right_high, right_high, right_low], axis=1),
        (((1,), (1,)), ((), ())),
        preferred_element_type=F32,
    )


def update_kernel(x_hbm, l_hbm, keep_ref, send_ref, x_buf, l_buf, total, sems):
    chunk = x_buf.shape[3]

    def copies(step):
        lanes = pl.ds(pl.multiple_of(step * chunk, chunk), chunk)
        return (
            pltpu.make_async_copy(l_hbm.at[:, :, :, lanes], l_buf.at[step], sems.at[step, 0]),
            pltpu.make_async_copy(x_hbm.at[:, :, lanes], x_buf.at[step], sems.at[step, 1]),
        )

    def begin(step, carry):
        for copy in copies(step):
            copy.start()
        return carry

    def multiply(step, carry):
        for copy in copies(step):
            copy.wait()
        left = jnp.concatenate([x_buf[step, 0], x_buf[step, 1]], axis=1)
        rows = []
        for panel in range(2):
            real, imag = l_buf[step, 0, panel], l_buf[step, 1, panel]
            rows.append(jnp.concatenate([real, imag], axis=1))
            rows.append(jnp.concatenate([-imag, real], axis=1))
        total[...] += dot_split(left, jnp.concatenate(rows, axis=0))
        return carry

    lax.fori_loop(0, CHUNKS, begin, 0)
    total[...] = jnp.zeros_like(total)
    lax.fori_loop(0, CHUNKS, multiply, 0)
    core = lax.axis_index("prow") % 2
    blocks, rows_each = keep_ref.shape[0], keep_ref.shape[1]
    for block in range(blocks):
        base = 2 * rows_each * block
        keep_ref[block] = total[pl.ds(pl.multiple_of(base + core * rows_each, 8), rows_each), :]
        send_ref[block] = total[pl.ds(pl.multiple_of(base + (1 - core) * rows_each, 8), rows_each), :]


def update(x_done, l_below, rows):
    _, sides, depth = x_done.shape
    width = l_below.shape[2]
    blocks = sides // (2 * rows)
    chunk = depth // CHUNKS
    half = jax.ShapeDtypeStruct((blocks, rows, 4 * width), F32)
    return pl.pallas_call(
        update_kernel,
        in_specs=[pl.BlockSpec(memory_space=pltpu.HBM)] * 2,
        out_specs=[VMEM] * 2,
        out_shape=[half, half],
        scratch_shapes=[
            pltpu.VMEM((CHUNKS, 2, sides, chunk), F32),
            pltpu.VMEM((CHUNKS, 2, 2, width, chunk), F32),
            pltpu.VMEM((sides, 4 * width), F32),
            pltpu.SemaphoreType.DMA((CHUNKS, 2)),
        ],
        compiler_params=pltpu.CompilerParams(vmem_limit_bytes=UPDATE_VMEM),
        cost_estimate=pl.CostEstimate(
            flops=2 * 3 * sides * 2 * depth * 4 * width, bytes_accessed=x_done.size * 4 + l_below.size * 4, transcendentals=0
        ),
    )(x_done, l_below)


def reduce_kernel(parts_ref, rhs_ref, zero_ref, spread_ref):
    rhs = jnp.concatenate([rhs_ref[part, :, panel, :] for panel in range(2) for part in range(2)], axis=1)
    total = parts_ref[0]
    for block in range(1, parts_ref.shape[0]):
        total = total + parts_ref[block]
    reduced = rhs - total
    half = reduced.shape[1] // 2
    zero_ref[...] = reduced[:, :half]
    spread(spread_ref, reduced[:, half:])


def weave(real, imag, conjugate):
    blocks = real.shape[1] // 128
    low = lax.broadcasted_iota(jnp.int32, (real.shape[0], 128), 1) < 64
    to_real, to_imag = [], []
    for block in range(blocks):
        lanes = slice(128 * block, 128 * (block + 1))
        re, im = real[:, lanes], imag[:, lanes]
        re_turned, im_turned = pltpu.roll(re, 64, 1), pltpu.roll(im, 64, 1)
        if conjugate:
            to_real += [jnp.where(low, re, im_turned), jnp.where(low, re_turned, im)]
            to_imag += [jnp.where(low, -im, re_turned), jnp.where(low, -im_turned, re)]
        else:
            to_real += [jnp.where(low, re, -im_turned), jnp.where(low, re_turned, -im)]
            to_imag += [jnp.where(low, im, re_turned), jnp.where(low, im_turned, re)]
    return jnp.concatenate([jnp.concatenate(to_real, axis=1), jnp.concatenate(to_imag, axis=1)], axis=0)


def apply_mat(gathered_ref, mat_ref):
    depth = mat_ref.shape[0] // 2
    high, low = split(jnp.concatenate([gathered_ref[block] for block in range(gathered_ref.shape[0])], axis=1))
    rows = high.shape[0]
    both = jnp.dot(jnp.concatenate([high, low], axis=0), mat_ref[:depth, :], preferred_element_type=F32)
    return both[:rows] + both[rows:] + jnp.dot(high, mat_ref[depth:, :], preferred_element_type=F32)


def store_split(out_ref, mat):
    depth = mat.shape[1]
    out_ref[:depth, :], out_ref[depth:, :] = split(mat.T)


def prepare_kernel(inv_ref, couple_ref, keep_ref, one_ref, coupling_ref, zero_ref, kept_ref):
    del keep_ref, kept_ref
    store_split(one_ref, weave(*masked(inv_ref, 1), False))
    store_split(coupling_ref, weave(couple_ref[0], couple_ref[1], True))
    store_split(zero_ref, weave(*masked(inv_ref, 0), False))


def masked(inv_ref, panel):
    shape = inv_ref.shape[2:]
    row_ids = lax.broadcasted_iota(jnp.int32, shape, 0) + lax.axis_index("pcol") * shape[0]
    upper = lax.broadcasted_iota(jnp.int32, shape, 1) >= row_ids
    return jnp.where(upper, inv_ref[0, panel], 0.0), jnp.where(upper, inv_ref[1, panel], 0.0)


def spread(out_ref, value):
    for target in range(out_ref.shape[0]):
        out_ref[target] = value


def one_kernel(gathered_ref, mat_ref, one_ref, spread_ref):
    one = apply_mat(gathered_ref, mat_ref)
    one_ref[...] = one
    spread(spread_ref, one)


def coupling_kernel(gathered_ref, mat_ref, zero_ref, spread_ref):
    spread(spread_ref, zero_ref[...] - apply_mat(gathered_ref, mat_ref))


def zero_kernel(gathered_ref, mat_ref, one_ref, out_ref):
    zero = apply_mat(gathered_ref, mat_ref)
    one = one_ref[...]
    width = out_ref.shape[3]
    for part in range(2):
        lanes = slice(part * width, (part + 1) * width)
        out_ref[part, :, 0, :] = zero[:, lanes]
        out_ref[part, :, 1, :] = one[:, lanes]


def call(kernel, out_shape, *args, out_spec=VMEM):
    return pl.pallas_call(
        kernel,
        in_specs=[VMEM] * len(args),
        out_specs=jax.tree.map(lambda array: out_spec, out_shape),
        out_shape=out_shape,
        compiler_params=pltpu.CompilerParams(vmem_limit_bytes=VMEM_LIMIT),
    )(*args)


def per_device(x_done, l_below, rhs_window, inv_diag, l_couple):
    columns = lax.axis_size("pcol")
    side_blocks = lax.axis_size("prow")
    rows, width = rhs_window.shape[1], l_below.shape[2]
    keep, send = update(x_done, l_below, rows)
    pair = [(i, i ^ 1) for i in range(side_blocks)]
    received = lax.ppermute(send, "prow", pair)
    mat = jax.ShapeDtypeStruct((4 * columns * width, 2 * width), BF)
    one_mat, coupling_mat, zero_mat, keep = pl.pallas_call(
        prepare_kernel,
        in_specs=[VMEM] * 3,
        out_specs=[VMEM] * 4,
        out_shape=[mat] * 3 + [jax.ShapeDtypeStruct(keep.shape, F32)],
        input_output_aliases={2: 3},
        compiler_params=pltpu.CompilerParams(vmem_limit_bytes=VMEM_LIMIT),
    )(inv_diag, l_couple, keep)
    levels = [[2 * z + k for z in range(side_blocks // 2)] for k in range(2)]
    parts = lax.all_to_all(keep + received, "prow", 0, 0, axis_index_groups=levels)
    flat = jax.ShapeDtypeStruct((rows, 2 * width), F32)
    wide = jax.ShapeDtypeStruct((columns, rows, 2 * width), F32)
    gather = lambda array: lax.all_to_all(array, "pcol", 0, 0)
    reduced_zero, to_send = call(reduce_kernel, [flat, wide], parts, rhs_window)
    one, to_send = call(one_kernel, [flat, wide], gather(to_send), one_mat)
    to_send = call(coupling_kernel, wide, gather(to_send), coupling_mat, reduced_zero)
    return call(zero_kernel, jax.ShapeDtypeStruct(rhs_window.shape, F32), gather(to_send), zero_mat, one)


def solution(mesh):
    placed = (
        P(None, None, "prow"),
        P(None, None, "pcol", "prow"),
        P(None, "prow", None, "pcol"),
        P(None, None, "pcol", None),
        P(None, "pcol", None),
    )
    return jax.shard_map(
        per_device,
        mesh=mesh,
        in_specs=placed,
        out_specs=P(None, "prow", None, "pcol"),
        check_vma=False,
    )
```

profile of v0, /device:TPU:8, one launch (start us, length us, event | category | flops | bytes accessed | tf_op | source)
XLA Modules:
  0.0 68.2 jit_solution(4819493003966110735)
XLA Ops:
  0.0 0.0 copy-start.1
  0.0 0.0 copy-start
  0.0 0.0 copy-start.2
  0.0 6.1 %shard_map.55 = (f32[8,32,256]{2,1,0:T(8,128)S(1)}, f32[8,32,256]{2,1,0:T(8,128)S(1)}) custom-call(f32[2,512,2048]{2,1,0:T(8,128)} %x_hbm.1, f32[2,2,64,2048]{3,2,1,0:T(8,128)} %l_hbm.1), custom_call_target="tpu_custom_call" | custom-call | flops 3221225472 | bytes 10485760 | tf_op jit(solution)/shard_map/pallas_call | solution.py:76
  6.1 0.1 collective-permute-start
  6.2 0.0 copy-done.1
  6.2 0.0 copy-done
  6.2 1.3 %shard_map.56 = (bf16[4096,128]{1,0:T(8,128)(2,1)S(1)}, bf16[4096,128]{1,0:T(8,128)(2,1)S(1)}, bf16[4096,128]{1,0:T(8,128)(2,1)S(1)}, f32[8,32,256]{2,1,0:T(8,128)S(1)}) custom-call(f32[2,2,64,1024]{3,2,1,0:T(8,128)S(1)} %copy-done, f32[2,64,1024]{2,1,0:T(8,128)S(1)} %copy-done.1, ...), custom_call_target="tpu_custom_call", output_to_operand_aliasing={{3}: (2, {})} | custom-call | tf_op jit(solution)/shard_map/pallas_call | solution.py:192
  7.5 0.2 collective-permute-done
  7.8 20.6 %all_to_all.20.parts_ref = f32[8,32,256]{2,1,0:T(8,128)S(1)} all-to-all(f32[8,32,256]{2,1,0:T(8,128)S(1)} %add.3), channel_id=1, replica_groups={{0,32,64,96,128,160,192,224},{16,48,80,112,144,176,208,240},{1,33,65,97..., dimensions={0} | all-to-all | bytes 524288 | tf_op jit(solution)/shard_map/all_to_all | solution.py:201
  28.4 0.0 copy-done.2
  28.4 0.1 shard_map.57
  28.5 14.3 %all_to_all.21.gathered_ref = f32[16,32,128]{2,1,0:T(8,128)S(1)} all-to-all(f32[16,32,128]{2,1,0:T(8,128)S(1)} %get-tuple-element.18), channel_id=1, replica_groups=mesh['prow'=16,'pcol'=16] {'pcol'}, dimensions={0} | all-to-all | bytes 524288 | tf_op jit(solution)/shard_map/all_to_all | solution.py:204
  42.8 0.3 shard_map.58
  43.1 11.8 %all_to_all.22.gathered_ref = f32[16,32,128]{2,1,0:T(8,128)S(1)} all-to-all(f32[16,32,128]{2,1,0:T(8,128)S(1)} %get-tuple-element.20), channel_id=1, replica_groups=mesh['prow'=16,'pcol'=16] {'pcol'}, dimensions={0} | all-to-all | bytes 524288 | tf_op jit(solution)/shard_map/all_to_all | solution.py:204
  55.0 0.3 shard_map.59
  55.3 11.9 %all_to_all.23.gathered_ref = f32[16,32,128]{2,1,0:T(8,128)S(1)} all-to-all(f32[16,32,128]{2,1,0:T(8,128)S(1)} %shard_map.59), channel_id=1, replica_groups=mesh['prow'=16,'pcol'=16] {'pcol'}, dimensions={0} | all-to-all | bytes 524288 | tf_op jit(solution)/shard_map/all_to_all | solution.py:204
  67.2 1.0 %shard_map.60 = f32[2,32,2,64]{3,2,1,0:T(2,128)} custom-call(f32[16,32,128]{2,1,0:T(8,128)S(1)} %all_to_all.23.gathered_ref, bf16[4096,128]{1,0:T(8,128)(2,1)S(1)} %get-tuple-element.23.mat_ref, f32[32,128]{1,0:T(8,128)S(1)} %get-tuple-element.24.one_ref), custom_call_target="tpu_custom_call" | custom-call | tf_op jit(solution)/shard_map/pallas_call | solution.py:175
  (1 shorter events, 0.0 us)
Async XLA Ops:
  0.0 6.2 %copy-start.1 = (f32[2,64,1024]{2,1,0:T(8,128)S(1)}, f32[2,64,1024]{2,1,0:T(8,128)}, u32[]{:S(2)}) copy-start(f32[2,64,1024]{2,1,0:T(8,128)} %couple_ref.1) | copy-start | bytes 1572868
  0.0 6.2 %copy-start = (f32[2,2,64,1024]{3,2,1,0:T(8,128)S(1)}, f32[2,2,64,1024]{3,2,1,0:T(8,128)}, u32[]{:S(2)}) copy-start(f32[2,2,64,1024]{3,2,1,0:T(8,128)} %inv_ref.1) | copy-start | bytes 3145732
  0.0 28.4 %copy-start.2 = (f32[2,32,2,64]{3,2,1,0:T(2,128)S(1)}, f32[2,32,2,64]{3,2,1,0:T(2,128)}, u32[]{:S(2)}) copy-start(f32[2,32,2,64]{3,2,1,0:T(2,128)} %rhs_ref.1) | copy-start | bytes 98308
  6.1 1.6 %collective-permute-start = (f32[8,32,256]{2,1,0:T(8,128)S(1)}, f32[8,32,256]{2,1,0:T(8,128)S(1)}, u32[]{:S(2)}, u32[]{:S(2)}) collective-permute-start(f32[8,32,256]{2,1,0:T(8,128)S(1)} %get-tuple-element.17), channel_id=1, source_target_pairs={{0,16},{16,0},{32,48},{48,32},{64,80},{80,64},{96,112},{112,96},{1... | collective-permute-start | bytes 786440 | tf_op jit(solution)/shard_map/ppermute | solution.py:190
where the time goes:
time: 68.5 us; the launch traced here: 68.2 us
  blocking collectives  58.7 us (86%)
  Pallas kernels  9.13 us (13%)
    all_to_all x3, blocking collectives, per_device(): gather = lambda array: lax.all_to_all(array, 'pcol', 0, 0)  38.1 us
    all_to_all x1, blocking collectives, per_device(): lax.all_to_all(keep + received, 'prow', 0, 0, axis_index_groups=levels)  20.6 us
    pallas_call x1, Pallas kernels, update(): pl.pallas_call(update_kernel, in_specs=[pl.BlockSpec(memory_space=pltpu.H...  6.09 us
    pallas_call x4, Pallas kernels, call(): pl.pallas_call(kernel, in_specs=[VMEM] * len(args), out_specs=jax.tree.ma...  1.73 us
  transfers between devices with their start and end apart: 1, of which 1 were waited for; matrix products, arithmetic and copies ran while one was open for 0% of the time, Pallas kernels for 2%

commit v1 on v0

v1 whole, which is shorter than its diff:
```python
import jax
import jax.numpy as jnp
from jax import lax
from jax.experimental import pallas as pl
from jax.experimental.pallas import tpu as pltpu
from jax.sharding import PartitionSpec as P

BF = jnp.bfloat16
F32 = jnp.float32
CHUNKS = 4
VMEM_LIMIT = 16 * 1024 * 1024
UPDATE_VMEM = 53 * 1024 * 1024
VMEM = pl.BlockSpec(memory_space=pltpu.VMEM)


def split(mat):
    high = mat.astype(BF)
    return high, (mat - high.astype(F32)).astype(BF)


def dot_split(left, right):
    left_high, left_low = split(left)
    right_high, right_low = split(right)
    return lax.dot_general(
        jnp.concatenate([left_high, left_low, left_high], axis=1),
        jnp.concatenate([right_high, right_high, right_low], axis=1),
        (((1,), (1,)), ((), ())),
        preferred_element_type=F32,
    )


def update_kernel(x_hbm, l_hbm, out_ref, x_buf, l_buf, total, sems):
    chunk = x_buf.shape[3]

    def copies(step):
        lanes = pl.ds(pl.multiple_of(step * chunk, chunk), chunk)
        return (
            pltpu.make_async_copy(l_hbm.at[:, :, :, lanes], l_buf.at[step], sems.at[step, 0]),
            pltpu.make_async_copy(x_hbm.at[:, :, lanes], x_buf.at[step], sems.at[step, 1]),
        )

    def begin(step, carry):
        for copy in copies(step):
            copy.start()
        return carry

    def multiply(step, carry):
        for copy in copies(step):
            copy.wait()
        left = jnp.concatenate([x_buf[step, 0], x_buf[step, 1]], axis=1)
        rows = []
        for panel in range(2):
            real, imag = l_buf[step, 0, panel], l_buf[step, 1, panel]
            rows.append(jnp.concatenate([real, imag], axis=1))
            rows.append(jnp.concatenate([-imag, real], axis=1))
        total[...] += dot_split(left, jnp.concatenate(rows, axis=0))
        return carry

    lax.fori_loop(0, CHUNKS, begin, 0)
    total[...] = jnp.zeros_like(total)
    lax.fori_loop(0, CHUNKS, multiply, 0)
    for level in range(out_ref.shape[0]):
        out_ref[level] = total[level * out_ref.shape[1] : (level + 1) * out_ref.shape[1], :]


def update(x_done, l_below, rows):
    _, sides, depth = x_done.shape
    width = l_below.shape[2]
    chunk = depth // CHUNKS
    return pl.pallas_call(
        update_kernel,
        in_specs=[pl.BlockSpec(memory_space=pltpu.HBM)] * 2,
        out_specs=VMEM,
        out_shape=jax.ShapeDtypeStruct((sides // rows, rows, 4 * width), F32),
        scratch_shapes=[
            pltpu.VMEM((CHUNKS, 2, sides, chunk), F32),
            pltpu.VMEM((CHUNKS, 2, 2, width, chunk), F32),
            pltpu.VMEM((sides, 4 * width), F32),
            pltpu.SemaphoreType.DMA((CHUNKS, 2)),
        ],
        compiler_params=pltpu.CompilerParams(vmem_limit_bytes=UPDATE_VMEM),
        cost_estimate=pl.CostEstimate(
            flops=2 * 3 * sides * 2 * depth * 4 * width, bytes_accessed=x_done.size * 4 + l_below.size * 4, transcendentals=0
        ),
    )(x_done, l_below)


def subtract_kernel(rhs_ref, total_ref, out_ref):
    del total_ref
    rows = rhs_ref.shape[1]
    rhs = jnp.concatenate([rhs_ref[part, :, panel, :] for panel in range(2) for part in range(2)], axis=1)
    device = lax.axis_index("prow")
    own = pl.ds(pl.multiple_of(device % 2 * rows, rows), rows)
    out_ref[device // 2, own, :] -= rhs


def add_kernel(mine_ref, other_ref, out_ref):
    del mine_ref
    out_ref[...] += other_ref[...]


def reduce_kernel(parts_ref, spread_ref):
    total = parts_ref[0]
    for block in range(1, parts_ref.shape[0]):
        total = total + parts_ref[block]
    spread(spread_ref, -total)


def weave(real, imag):
    blocks = real.shape[1] // 128
    low = lax.broadcasted_iota(jnp.int32, (real.shape[0], 128), 1) < 64
    to_real, to_imag = [], []
    for block in range(blocks):
        lanes = slice(128 * block, 128 * (block + 1))
        re, im = real[:, lanes], imag[:, lanes]
        re_turned, im_turned = pltpu.roll(re, 64, 1), pltpu.roll(im, 64, 1)
        to_real += [jnp.where(low, re, -im_turned), jnp.where(low, re_turned, -im)]
        to_imag += [jnp.where(low, im, re_turned), jnp.where(low, im_turned, re)]
    return jnp.concatenate([jnp.concatenate(to_real, axis=1), jnp.concatenate(to_imag, axis=1)], axis=0)


def apply_mat(gathered_ref, lanes, mat_high, mat_low):
    blocks = [gathered_ref[block, :, lanes] for block in range(gathered_ref.shape[0])]
    high, low = split(jnp.concatenate(blocks, axis=1))
    rows = high.shape[0]
    both = jnp.dot(jnp.concatenate([high, low], axis=0), mat_high, preferred_element_type=F32)
    return both[:rows] + both[rows:] + jnp.dot(high, mat_low, preferred_element_type=F32)


def masked(inv_ref, panel):
    shape = inv_ref.shape[2:]
    row_ids = lax.broadcasted_iota(jnp.int32, shape, 0) + lax.axis_index("pcol") * shape[0]
    upper = lax.broadcasted_iota(jnp.int32, shape, 1) >= row_ids
    return jnp.where(upper, inv_ref[0, panel], 0.0), jnp.where(upper, inv_ref[1, panel], 0.0)


def spread(out_ref, value):
    for target in range(out_ref.shape[0]):
        out_ref[target] = value


def blank(out_ref):
    out_ref[0] = jnp.zeros(out_ref.shape[1:], F32)


def woven(real, imag):
    return split(weave(real, imag).T)


def one_kernel(gathered_ref, inv_ref, ship_ref, held_ref, blank_ref):
    blank(blank_ref)
    half, rows = gathered_ref.shape[2] // 2, held_ref.shape[1]
    for place, panel in enumerate((0, 1)):
        lanes = slice(panel * half, (panel + 1) * half)
        applied = apply_mat(gathered_ref, lanes, *woven(*masked(inv_ref, panel)))
        ship_ref[place], held_ref[place] = applied[:rows], applied[rows:]


def spread_kernel(mine_ref, other_ref, own_ref, spread_ref):
    own = jnp.where(lax.axis_index("prow") % 2 == 1, mine_ref[...], other_ref[...])
    own_ref[...] = own
    spread(spread_ref, own[1])


def columns_kernel(couple_ref, after_ref, spread_ref):
    del after_ref
    width = spread_ref.shape[3]
    lanes = pl.ds(pl.multiple_of(lax.axis_index("prow") // 2 * width, width), width)
    for target in range(spread_ref.shape[0]):
        spread_ref[target] = couple_ref[:, :, lanes]


def product_kernel(inv_ref, columns_ref, spread_ref, ship_ref, held_ref):
    blank(ship_ref)
    blank(held_ref)
    left = jnp.concatenate(masked(inv_ref, 0), axis=0)
    count, rows = columns_ref.shape[0], left.shape[0] // 2
    right = jnp.concatenate(
        [jnp.concatenate([columns_ref[block, part] for block in range(count)], axis=0) for part in range(2)], axis=1
    )
    left_high, left_low = split(left)
    right_high, right_low = split(right)
    both = jnp.dot(jnp.concatenate([left_high, left_low], axis=0), right_high, preferred_element_type=F32)
    product = both[: 2 * rows] + both[2 * rows :] + jnp.dot(left_high, right_low, preferred_element_type=F32)
    half = product.shape[1] // 2
    for target in range(spread_ref.shape[0]):
        spread_ref[target, 0] = product[:rows, :half] + product[rows:, half:]
        spread_ref[target, 1] = product[rows:, :half] - product[:rows, half:]


def zero_kernel(gathered_ref, mine_ref, other_ref, own_ref, out_ref):
    upper = lax.axis_index("prow") % 2 == 1
    product = jnp.where(upper, other_ref[...], mine_ref[...])
    levels, width = product.shape[0] // 2, out_ref.shape[3]
    real = jnp.concatenate([product[2 * level] for level in range(levels)], axis=1)
    imag = jnp.concatenate([product[2 * level + 1] for level in range(levels)], axis=1)
    zero = own_ref[0] - apply_mat(gathered_ref, slice(None), *woven(real, imag))
    for panel, solved in enumerate((zero, own_ref[1])):
        for part in range(2):
            out_ref[part, :, panel, :] = solved[:, part * width : (part + 1) * width]


def blank_kernel(after_ref, out_ref):
    del after_ref
    blank(out_ref)


def call(kernel, out_shape, *args, aliases={}):
    return pl.pallas_call(
        kernel,
        in_specs=[VMEM] * len(args),
        out_specs=jax.tree.map(lambda array: VMEM, out_shape),
        out_shape=out_shape,
        input_output_aliases=aliases,
        compiler_params=pltpu.CompilerParams(vmem_limit_bytes=VMEM_LIMIT),
    )(*args)


def per_device(x_done, l_below, rhs_window, inv_diag, l_couple):
    columns, levels = lax.axis_size("pcol"), lax.axis_size("prow") // 2
    rows, width = 2 * rhs_window.shape[1], l_below.shape[2]
    block = inv_diag.shape[3] // levels
    upper = lax.axis_index("prow") % 2 == 1
    swap = [(device, device ^ 1) for device in range(2 * levels)]
    same_core = [[2 * level + core for level in range(levels)] for core in range(2)]
    array = lambda *shape: jax.ShapeDtypeStruct(shape, F32)
    over_columns = lambda value: lax.all_to_all(value, "pcol", 0, 0)
    over_levels = lambda value: lax.all_to_all(value, "prow", 0, 0, axis_index_groups=same_core)

    total = update(x_done, l_below, rows)
    total = call(subtract_kernel, array(*total.shape), rhs_window, total, aliases={1: 0})
    received = lax.ppermute(total, "prow", swap)
    parts = array(columns, 2, width, block)

    share = lambda l_couple, after: over_columns(call(columns_kernel, parts, l_couple, after))
    skip = lambda l_couple, after: call(blank_kernel, parts, after)
    gathered = lax.cond(upper, skip, share, l_couple, total)
    summed = call(add_kernel, array(*total.shape), total, received, aliases={0: 0})
    own = array(2, rows // 2, 2 * width)
    whole = array(columns, rows, 2 * width)

    def solve(summed, inv_diag, gathered):
        del gathered
        reduced = call(reduce_kernel, array(columns, rows, 4 * width), over_levels(summed))
        return tuple(call(one_kernel, [own, own, whole], over_columns(reduced), inv_diag))

    def multiply(summed, inv_diag, gathered):
        del summed
        product = array(levels, 2, width, block)
        product, ship, held = call(product_kernel, [product, own, own], inv_diag, gathered)
        return ship, held, over_levels(product).reshape(whole.shape)

    ship, held, product = lax.cond(upper, solve, multiply, summed, inv_diag, gathered)
    shipped = lax.ppermute(ship, "prow", swap)
    other = lax.ppermute(product, "prow", swap)
    held, one = call(spread_kernel, [own, array(columns, rows // 2, 2 * width)], held, shipped)
    return call(zero_kernel, array(*rhs_window.shape), over_columns(one), product, other, held)


def solution(mesh):
    placed = (
        P(None, None, "prow"),
        P(None, None, "pcol", "prow"),
        P(None, "prow", None, "pcol"),
        P(None, None, "pcol", None),
        P(None, "pcol", None),
    )
    return jax.shard_map(
        per_device,
        mesh=mesh,
        in_specs=placed,
        out_specs=P(None, "prow", None, "pcol"),
        check_vma=False,
    )
```

time: 68.5 us -> 63.8 us (0.931)
  the two profiles are of different devices: /device:TPU:8 before, /device:TPU:1 now
where the time goes in v1:
time: 63.8 us; the launch traced here: 63.6 us
  blocking collectives  47.5 us (74%)
  Pallas kernels  9 us (14%)
  starting transfers between devices  3.96 us (6%)
  waiting for transfers between devices  3.11 us (5%)
    all_to_all x2, blocking collectives, per_device(): over_columns = lambda value: lax.all_to_all(value, 'pcol', 0, 0)  29 us
    all_to_all x1, blocking collectives, per_device(): lax.all_to_all(value, 'prow', 0, 0, axis_index_groups=same_core)  18.4 us
    pallas_call x1, Pallas kernels, update(): pl.pallas_call(update_kernel, in_specs=[pl.BlockSpec(memory_space=pltpu.H...  6.08 us
    ppermute x1, starting transfers between devices, per_device(): received = lax.ppermute(total, 'prow', swap)  3.31 us
    pallas_call x7, Pallas kernels, call(): pl.pallas_call(kernel, in_specs=[VMEM] * len(args), out_specs=jax.tree.ma...  2.92 us
    ppermute x1, waiting for transfers between devices, per_device(): shipped = lax.ppermute(ship, 'prow', swap)  1.58 us
    ppermute x1, waiting for transfers between devices, per_device(): received = lax.ppermute(total, 'prow', swap)  1.52 us
  transfers between devices with their start and end apart: 3, of which 2 were waited for; matrix products, arithmetic and copies ran while one was open for 0% of the time, Pallas kernels for 0%

profile of v1, /device:TPU:1, one launch (start us, length us, event | category | flops | bytes accessed | tf_op | source)
XLA Modules:
  0.0 63.6 jit_solution(17947157351951609984)
XLA Ops:
  0.0 0.0 copy-start
  0.0 0.0 copy-start.2
  0.0 0.0 copy-start.1
  0.0 6.1 %shard_map.56.total_ref = f32[8,64,256]{2,1,0:T(8,128)S(1)} custom-call(f32[2,512,2048]{2,1,0:T(8,128)} %x_hbm.1, f32[2,2,64,2048]{3,2,1,0:T(8,128)} %l_hbm.1), custom_call_target="tpu_custom_call" | custom-call | flops 3221225472 | bytes 10485760 | tf_op jit(solution)/shard_map/pallas_call | solution.py:70
  6.1 0.0 copy-done
  6.1 0.1 shard_map.57.mine_ref
  6.2 3.3 %collective-permute-start = (f32[8,64,256]{2,1,0:T(8,128)S(1)}, f32[8,64,256]{2,1,0:T(8,128)S(1)}, u32[]{:S(2)}, u32[]{:S(2)}) collective-permute-start(f32[8,64,256]{2,1,0:T(8,128)S(1)} %shard_map.57.mine_ref), channel_id=1, source_target_pairs={{0,16},{16,0},{32,48},{48,32},{64,80},{80,64},{96,112},{112,96},{1... | collective-permute-start | bytes 1572872 | tf_op jit(solution)/shard_map/ppermute | solution.py:232
  9.5 0.0 copy-done.2
  9.5 1.5 %collective-permute-done.other_ref = f32[8,64,256]{2,1,0:T(8,128)S(1)} collective-permute-done((f32[8,64,256]{2,1,0:T(8,128)S(1)}, f32[8,64,256]{2,1,0:T(8,128)S(1)}, u32[]{:S(2)}, u32[]{:S(2)}) %collective-permute-start) | collective-permute-done | bytes 524320 | tf_op jit(solution)/shard_map/ppermute | solution.py:232
  11.0 0.1 shard_map.58
  11.1 0.0 copy-done.1
  11.1 38.0 %conditional.3 = ((f32[2,32,128]{2,1,0:T(8,128)S(1)}, f32[2,32,128]{2,1,0:T(8,128)S(1)}, f32[16,64,128]{2,1,0:T(8,128)S(1)})) conditional(s32[]{:T(128)} %convert_element_type.4, (f32[2,2,64,1024]{3,2,1,0:T(8,128)S(1)}, f32[16,2,64,128]{3,2,1,0:T(8,128)S(1)}) %tuple.27, (f32[8,64,256]{2,1,0:T(8,128)S(1)}, f32[2,2,64,1024]{3,2,1,0:T(8,128)S(1)}) %tuple.28), branch_computations={%region_2.3_spmd, %region_3.4_spmd} | conditional | bytes 3145736 | solution.py:253
  11.1 18.4 %all_to_all.23.parts_ref = f32[8,64,256]{2,1,0:T(8,128)S(1)} all-to-all(f32[8,64,256]{2,1,0:T(8,128)S(1)} %get-tuple-element.28), channel_id=1, replica_groups={{0,32,64,96,128,160,192,224},{16,48,80,112,144,176,208,240},{1,33,65,97..., dimensions={0} | all-to-all | bytes 1048576 | tf_op jit(solution)/shard_map/cond/branch_1_fun/all_to_all | solution.py:228
  29.5 0.1 branch_1_fun.4
  29.6 18.3 %all_to_all.24.gathered_ref = f32[16,64,256]{2,1,0:T(8,128)S(1)} all-to-all(f32[16,64,256]{2,1,0:T(8,128)S(1)} %branch_1_fun.4), channel_id=1, replica_groups=mesh['prow'=16,'pcol'=16] {'pcol'}, dimensions={0} | all-to-all | bytes 2097152 | tf_op jit(solution)/shard_map/cond/branch_1_fun/all_to_all | solution.py:227
  47.9 1.2 %branch_1_fun.5 = (f32[2,32,128]{2,1,0:T(8,128)S(1)}, f32[2,32,128]{2,1,0:T(8,128)S(1)}, f32[16,64,128]{2,1,0:T(8,128)S(1)}) custom-call(f32[16,64,256]{2,1,0:T(8,128)S(1)} %all_to_all.24.gathered_ref, f32[2,2,64,1024]{3,2,1,0:T(8,128)S(1)} %get-tuple-element.29.inv_ref), custom_call_target="tpu_custom_call" | custom-call | tf_op jit(solution)/shard_map/cond/branch_1_fun/pallas_call | solution.py:209
  49.1 0.6 %collective-permute-start.2 = (f32[16,64,128]{2,1,0:T(8,128)S(1)}, f32[16,64,128]{2,1,0:T(8,128)S(1)}, u32[]{:S(2)}, u32[]{:S(2)}) collective-permute-start(f32[16,64,128]{2,1,0:T(8,128)S(1)} %get-tuple-element.38.mine_ref), channel_id=1, source_target_pairs={{0,16},{16,0},{32,48},{48,32},{64,80},{80,64},{96,112},{112,96},{1... | collective-permute-start | bytes 1572872 | tf_op jit(solution)/shard_map/ppermute | solution.py:255
  49.8 0.0 collective-permute-start.1
  49.8 1.6 %collective-permute-done.1.other_ref = f32[2,32,128]{2,1,0:T(8,128)S(1)} collective-permute-done((f32[2,32,128]{2,1,0:T(8,128)S(1)}, f32[2,32,128]{2,1,0:T(8,128)S(1)}, u32[]{:S(2)}, u32[]{:S(2)}) %collective-permute-start.1) | collective-permute-done | bytes 32800 | tf_op jit(solution)/shard_map/ppermute | solution.py:254
  51.4 10.7 %all_to_all.25.gathered_ref = f32[16,32,128]{2,1,0:T(8,128)S(1)} all-to-all(f32[16,32,128]{2,1,0:T(8,128)S(1)} %get-tuple-element.37), channel_id=1, replica_groups=mesh['prow'=16,'pcol'=16] {'pcol'}, dimensions={0} | all-to-all | bytes 524288 | tf_op jit(solution)/shard_map/all_to_all | solution.py:227
  62.1 0.0 collective-permute-done.2.other_ref
  62.1 1.5 %shard_map.60 = f32[2,32,2,64]{3,2,1,0:T(2,128)} custom-call(f32[16,32,128]{2,1,0:T(8,128)S(1)} %all_to_all.25.gathered_ref, f32[16,64,128]{2,1,0:T(8,128)S(1)} %get-tuple-element.38.mine_ref, f32[16,64,128]{2,1,0:T(8,128)S(1)} %collective-permute-done.2.other_ref, f32[2,32,128]{2,1,0:T(8,128)S(1)} %get-tuple-element.39.own_ref), custom_call_target="tpu_custom_call" | custom-call | tf_op jit(solution)/shard_map/pallas_call | solution.py:209
  (3 shorter events, 0.0 us)
Async XLA Ops:
  0.0 6.1 %copy-start = (f32[2,32,2,64]{3,2,1,0:T(2,128)S(1)}, f32[2,32,2,64]{3,2,1,0:T(2,128)}, u32[]{:S(2)}) copy-start(f32[2,32,2,64]{3,2,1,0:T(2,128)} %rhs_ref.1) | copy-start | bytes 98308
  0.0 9.5 %copy-start.2 = (f32[2,64,1024]{2,1,0:T(8,128)S(1)}, f32[2,64,1024]{2,1,0:T(8,128)}, u32[]{:S(2)}) copy-start(f32[2,64,1024]{2,1,0:T(8,128)} %param.13) | copy-start | bytes 1572868
  0.0 11.1 %copy-start.1 = (f32[2,2,64,1024]{3,2,1,0:T(8,128)S(1)}, f32[2,2,64,1024]{3,2,1,0:T(8,128)}, u32[]{:S(2)}) copy-start(f32[2,2,64,1024]{3,2,1,0:T(8,128)} %param.12) | copy-start | bytes 3145732
  6.2 4.8 %collective-permute-start = (f32[8,64,256]{2,1,0:T(8,128)S(1)}, f32[8,64,256]{2,1,0:T(8,128)S(1)}, u32[]{:S(2)}, u32[]{:S(2)}) collective-permute-start(f32[8,64,256]{2,1,0:T(8,128)S(1)} %shard_map.57.mine_ref), channel_id=1, source_target_pairs={{0,16},{16,0},{32,48},{48,32},{64,80},{80,64},{96,112},{112,96},{1... | collective-permute-start | bytes 1572872 | tf_op jit(solution)/shard_map/ppermute | solution.py:232
  49.1 13.0 %collective-permute-start.2 = (f32[16,64,128]{2,1,0:T(8,128)S(1)}, f32[16,64,128]{2,1,0:T(8,128)S(1)}, u32[]{:S(2)}, u32[]{:S(2)}) collective-permute-start(f32[16,64,128]{2,1,0:T(8,128)S(1)} %get-tuple-element.38.mine_ref), channel_id=1, source_target_pairs={{0,16},{16,0},{32,48},{48,32},{64,80},{80,64},{96,112},{112,96},{1... | collective-permute-start | bytes 1572872 | tf_op jit(solution)/shard_map/ppermute | solution.py:255
  49.8 1.6 %collective-permute-start.1 = (f32[2,32,128]{2,1,0:T(8,128)S(1)}, f32[2,32,128]{2,1,0:T(8,128)S(1)}, u32[]{:S(2)}, u32[]{:S(2)}) collective-permute-start(f32[2,32,128]{2,1,0:T(8,128)S(1)} %get-tuple-element.36), channel_id=1, source_target_pairs={{0,16},{16,0},{32,48},{48,32},{64,80},{80,64},{96,112},{112,96},{1... | collective-permute-start | bytes 98312 | tf_op jit(solution)/shard_map/ppermute | solution.py:254

commit v2 on v1

--- a/solution.py
+++ b/solution.py
@@ -147,16 +147,25 @@
     return split(weave(real, imag).T)
 
 
-def one_kernel(gathered_ref, inv_ref, ship_ref, held_ref, blank_ref):
+def ready_kernel(inv_ref, after_ref, out_ref):
+    del after_ref
+    mat = weave(*masked(inv_ref, 1)).T
+    count = mat.shape[0] // out_ref.shape[0]
+    for block in range(out_ref.shape[0]):
+        out_ref[block] = mat[block * count : (block + 1) * count]
+
+
+def one_kernel(gathered_ref, ready_ref, inv_ref, ship_ref, held_ref, blank_ref):
     blank(blank_ref)
     half, rows = gathered_ref.shape[2] // 2, held_ref.shape[1]
-    for place, panel in enumerate((0, 1)):
-        lanes = slice(panel * half, (panel + 1) * half)
-        applied = apply_mat(gathered_ref, lanes, *woven(*masked(inv_ref, panel)))
-        ship_ref[place], held_ref[place] = applied[:rows], applied[rows:]
-
-
-def spread_kernel(mine_ref, other_ref, own_ref, spread_ref):
+    ready = jnp.concatenate([ready_ref[block] for block in range(ready_ref.shape[0])], axis=0)
+    for panel, mats in enumerate((woven(*masked(inv_ref, 0)), split(ready))):
+        applied = apply_mat(gathered_ref, slice(panel * half, (panel + 1) * half), *mats)
+        ship_ref[panel], held_ref[panel] = applied[:rows], applied[rows:]
+
+
+def spread_kernel(mine_ref, other_ref, product_ref, own_ref, spread_ref, kept_ref):
+    del product_ref, kept_ref
     own = jnp.where(lax.axis_index("prow") % 2 == 1, mine_ref[...], other_ref[...])
     own_ref[...] = own
     spread(spread_ref, own[1])
@@ -164,10 +173,10 @@
 
 def columns_kernel(couple_ref, after_ref, spread_ref):
     del after_ref
-    width = spread_ref.shape[3]
+    width = spread_ref.shape[2]
     lanes = pl.ds(pl.multiple_of(lax.axis_index("prow") // 2 * width, width), width)
-    for target in range(spread_ref.shape[0]):
-        spread_ref[target] = couple_ref[:, :, lanes]
+    both = jnp.concatenate([couple_ref[0, :, lanes], couple_ref[1, :, lanes]], axis=0)
+    spread(spread_ref, both)
 
 
 def product_kernel(inv_ref, columns_ref, spread_ref, ship_ref, held_ref):
@@ -176,7 +185,11 @@
     left = jnp.concatenate(masked(inv_ref, 0), axis=0)
     count, rows = columns_ref.shape[0], left.shape[0] // 2
     right = jnp.concatenate(
-        [jnp.concatenate([columns_ref[block, part] for block in range(count)], axis=0) for part in range(2)], axis=1
+        [
+            jnp.concatenate([columns_ref[block, part * rows : (part + 1) * rows] for block in range(count)], axis=0)
+            for part in range(2)
+        ],
+        axis=1,
     )
     left_high, left_low = split(left)
     right_high, right_low = split(right)
@@ -188,21 +201,35 @@
         spread_ref[target, 1] = product[rows:, :half] - product[:rows, half:]
 
 
-def zero_kernel(gathered_ref, mine_ref, other_ref, own_ref, out_ref):
+def product_mats(product_ref):
+    levels = product_ref.shape[0] // 2
+    real = jnp.concatenate([product_ref[2 * level] for level in range(levels)], axis=1)
+    imag = jnp.concatenate([product_ref[2 * level + 1] for level in range(levels)], axis=1)
+    return woven(real, imag)
+
+
+def weave_kernel(product_ref, mat_ref):
+    depth = mat_ref.shape[0] // 2
+    mat_ref[:depth, :], mat_ref[depth:, :] = product_mats(product_ref)
+
+
+def zero_kernel(gathered_ref, mat_ref, other_ref, own_ref, out_ref):
     upper = lax.axis_index("prow") % 2 == 1
-    product = jnp.where(upper, other_ref[...], mine_ref[...])
-    levels, width = product.shape[0] // 2, out_ref.shape[3]
-    real = jnp.concatenate([product[2 * level] for level in range(levels)], axis=1)
-    imag = jnp.concatenate([product[2 * level + 1] for level in range(levels)], axis=1)
-    zero = own_ref[0] - apply_mat(gathered_ref, slice(None), *woven(real, imag))
-    for panel, solved in enumerate((zero, own_ref[1])):
-        for part in range(2):
-            out_ref[part, :, panel, :] = solved[:, part * width : (part + 1) * width]
-
-
-def blank_kernel(after_ref, out_ref):
-    del after_ref
-    blank(out_ref)
+    depth, width = mat_ref.shape[0] // 2, out_ref.shape[3]
+
+    def finish(mat_high, mat_low):
+        zero = own_ref[0] - apply_mat(gathered_ref, slice(None), mat_high, mat_low)
+        for panel, solved in enumerate((zero, own_ref[1])):
+            for part in range(2):
+                out_ref[part, :, panel, :] = solved[:, part * width : (part + 1) * width]
+
+    @pl.when(upper)
+    def _():
+        finish(*product_mats(other_ref))
+
+    @pl.when(jnp.logical_not(upper))
+    def _():
+        finish(mat_ref[:depth, :], mat_ref[depth:, :])
 
 
 def call(kernel, out_shape, *args, aliases={}):
@@ -230,19 +257,18 @@
     total = update(x_done, l_below, rows)
     total = call(subtract_kernel, array(*total.shape), rhs_window, total, aliases={1: 0})
     received = lax.ppermute(total, "prow", swap)
-    parts = array(columns, 2, width, block)
-
-    share = lambda l_couple, after: over_columns(call(columns_kernel, parts, l_couple, after))
-    skip = lambda l_couple, after: call(blank_kernel, parts, after)
-    gathered = lax.cond(upper, skip, share, l_couple, total)
+    parts = array(columns, 2 * width, block)
+
+    share = lambda l_couple, inv_diag, after: over_columns(call(columns_kernel, parts, l_couple, after))
+    ready = lambda l_couple, inv_diag, after: call(ready_kernel, parts, inv_diag, after)
+    gathered = lax.cond(upper, ready, share, l_couple, inv_diag, total)
     summed = call(add_kernel, array(*total.shape), total, received, aliases={0: 0})
     own = array(2, rows // 2, 2 * width)
     whole = array(columns, rows, 2 * width)
 
-    def solve(summed, inv_diag, gathered):
-        del gathered
+    def solve(summed, inv_diag, ready):
         reduced = call(reduce_kernel, array(columns, rows, 4 * width), over_levels(summed))
-        return tuple(call(one_kernel, [own, own, whole], over_columns(reduced), inv_diag))
+        return tuple(call(one_kernel, [own, own, whole], over_columns(reduced), ready, inv_diag))
 
     def multiply(summed, inv_diag, gathered):
         del summed
@@ -252,9 +278,12 @@
 
     ship, held, product = lax.cond(upper, solve, multiply, summed, inv_diag, gathered)
     shipped = lax.ppermute(ship, "prow", swap)
+    mat = jax.ShapeDtypeStruct((4 * columns * width, 2 * width), BF)
+    mat = call(weave_kernel, mat, product)
+    one = array(columns, rows // 2, 2 * width)
+    held, one, product = call(spread_kernel, [own, one, whole], held, shipped, product, aliases={2: 2})
     other = lax.ppermute(product, "prow", swap)
-    held, one = call(spread_kernel, [own, array(columns, rows // 2, 2 * width)], held, shipped)
-    return call(zero_kernel, array(*rhs_window.shape), over_columns(one), product, other, held)
+    return call(zero_kernel, array(*rhs_window.shape), over_columns(one), mat, other, held)
 
 
 def solution(mesh):

time: 63.8 us -> 63.5 us (level)
  waiting for transfers between devices: 3.11 us -> 1.4 us
  Pallas kernels: 9 us -> 9.81 us
  starting transfers between devices: 3.96 us -> 4.6 us
    ppermute x1, waiting for transfers between devices: 1.58 us -> 0.36 us  [per_device(): shipped = lax.ppermute(ship, 'prow', swap)]
    ppermute x1, starting transfers between devices: 0.01 us -> 0.85 us  [per_device(): shipped = lax.ppermute(ship, 'prow', swap)]
    pallas_call x7 -> x8, Pallas kernels: 2.92 us -> 3.73 us  [call(): pl.pallas_call(kernel, in_specs=[VMEM] * len(args), out_specs=jax.tree.ma...]
  transfers between devices with their start and end apart: 3 -> 3, of which waited for: 2 -> 2; matrix products, arithmetic and copies ran while one was open for 0% -> 0% of each run, Pallas kernels for 0% -> 2%
where the time goes in v2:
time: 63.5 us; the launch traced here: 63.3 us
  blocking collectives  47.4 us (75%)
  Pallas kernels  9.81 us (15%)
  starting transfers between devices  4.6 us (7%)
  waiting for transfers between devices  1.4 us (2%)
    all_to_all x2, blocking collectives, per_device(): over_columns = lambda value: lax.all_to_all(value, 'pcol', 0, 0)  29 us
    all_to_all x1, blocking collectives, per_device(): lax.all_to_all(value, 'prow', 0, 0, axis_index_groups=same_core)  18.4 us
    pallas_call x1, Pallas kernels, update(): pl.pallas_call(update_kernel, in_specs=[pl.BlockSpec(memory_space=pltpu.H...  6.07 us
    pallas_call x8, Pallas kernels, call(): pl.pallas_call(kernel, in_specs=[VMEM] * len(args), out_specs=jax.tree.ma...  3.73 us
    ppermute x1, starting transfers between devices, per_device(): received = lax.ppermute(total, 'prow', swap)  3.31 us
  transfers between devices with their start and end apart: 3, of which 2 were waited for; matrix products, arithmetic and copies ran while one was open for 0% of the time, Pallas kernels for 2%

profile of v2, /device:TPU:1, one launch (start us, length us, event | category | flops | bytes accessed | tf_op | source)
XLA Modules:
  0.0 63.3 jit_solution(3452439266187820794)
XLA Ops:
  0.0 0.0 copy-start
  0.0 0.0 copy-start.1
  0.0 0.0 copy-start.2
  0.0 6.1 %shard_map.56.total_ref = f32[8,64,256]{2,1,0:T(8,128)S(1)} custom-call(f32[2,512,2048]{2,1,0:T(8,128)} %x_hbm.1, f32[2,2,64,2048]{3,2,1,0:T(8,128)} %l_hbm.1), custom_call_target="tpu_custom_call" | custom-call | flops 3221225472 | bytes 10485760 | tf_op jit(solution)/shard_map/pallas_call | solution.py:70
  6.1 0.0 copy-done
  6.1 0.1 shard_map.57.mine_ref
  6.2 3.3 %collective-permute-start = (f32[8,64,256]{2,1,0:T(8,128)S(1)}, f32[8,64,256]{2,1,0:T(8,128)S(1)}, u32[]{:S(2)}, u32[]{:S(2)}) collective-permute-start(f32[8,64,256]{2,1,0:T(8,128)S(1)} %shard_map.57.mine_ref), channel_id=1, source_target_pairs={{0,16},{16,0},{32,48},{48,32},{64,80},{80,64},{96,112},{112,96},{1... | collective-permute-start | bytes 1572872 | tf_op jit(solution)/shard_map/ppermute | solution.py:259
  9.5 0.0 copy-done.1
  9.5 0.0 copy-done.2
  9.5 0.5 conditional.2
  9.5 0.5 branch_1_fun.3
  10.0 1.0 %collective-permute-done.other_ref = f32[8,64,256]{2,1,0:T(8,128)S(1)} collective-permute-done((f32[8,64,256]{2,1,0:T(8,128)S(1)}, f32[8,64,256]{2,1,0:T(8,128)S(1)}, u32[]{:S(2)}, u32[]{:S(2)}) %collective-permute-start) | collective-permute-done | bytes 524320 | tf_op jit(solution)/shard_map/ppermute | solution.py:259
  11.0 0.1 shard_map.58
  11.1 37.8 %conditional.3 = ((f32[2,32,128]{2,1,0:T(8,128)S(1)}, f32[2,32,128]{2,1,0:T(8,128)S(1)}, f32[16,64,128]{2,1,0:T(8,128)S(1)})) conditional(s32[]{:T(128)} %convert_element_type.4, (f32[2,2,64,1024]{3,2,1,0:T(8,128)S(1)}, f32[16,128,128]{2,1,0:T(8,128)S(1)}) %tuple.29, (f32[8,64,256]{2,1,0:T(8,128)S(1)}, f32[16,128,128]{2,1,0:T(8,128)S(1)}, ...), branch_computations={%region_2.3_spmd, %region_3.4_spmd} | conditional | bytes 3145736 | solution.py:279
  11.1 18.4 %all_to_all.23.parts_ref = f32[8,64,256]{2,1,0:T(8,128)S(1)} all-to-all(f32[8,64,256]{2,1,0:T(8,128)S(1)} %get-tuple-element.35), channel_id=1, replica_groups={{0,32,64,96,128,160,192,224},{16,48,80,112,144,176,208,240},{1,33,65,97..., dimensions={0} | all-to-all | bytes 1048576 | tf_op jit(solution)/shard_map/cond/branch_1_fun/all_to_all | solution.py:255
  29.5 0.1 branch_1_fun.4
  29.6 18.3 %all_to_all.24.gathered_ref = f32[16,64,256]{2,1,0:T(8,128)S(1)} all-to-all(f32[16,64,256]{2,1,0:T(8,128)S(1)} %branch_1_fun.4), channel_id=1, replica_groups=mesh['prow'=16,'pcol'=16] {'pcol'}, dimensions={0} | all-to-all | bytes 2097152 | tf_op jit(solution)/shard_map/cond/branch_1_fun/all_to_all | solution.py:254
  47.9 1.0 %branch_1_fun.5 = (f32[2,32,128]{2,1,0:T(8,128)S(1)}, f32[2,32,128]{2,1,0:T(8,128)S(1)}, f32[16,64,128]{2,1,0:T(8,128)S(1)}) custom-call(f32[16,64,256]{2,1,0:T(8,128)S(1)} %all_to_all.24.gathered_ref, f32[16,128,128]{2,1,0:T(8,128)S(1)} %get-tuple-element.36.ready_ref, f32[2,2,64,1024]{3,2,1,0:T(8,128)S(1)} %get-tuple-element.37.inv_ref), custom_call_target="tpu_custom_call" | custom-call | tf_op jit(solution)/shard_map/cond/branch_1_fun/pallas_call | solution.py:236
  48.9 0.8 %collective-permute-start.1 = (f32[2,32,128]{2,1,0:T(8,128)S(1)}, f32[2,32,128]{2,1,0:T(8,128)S(1)}, u32[]{:S(2)}, u32[]{:S(2)}) collective-permute-start(f32[2,32,128]{2,1,0:T(8,128)S(1)} %get-tuple-element.45), channel_id=1, source_target_pairs={{0,16},{16,0},{32,48},{48,32},{64,80},{80,64},{96,112},{112,96},{1... | collective-permute-start | bytes 98312 | tf_op jit(solution)/shard_map/ppermute | solution.py:280
  49.8 0.5 shard_map.60.mat_ref
  50.3 0.4 collective-permute-done.1.other_ref
  50.7 0.4 collective-permute-start.2
  51.1 10.7 %all_to_all.25.gathered_ref = f32[16,32,128]{2,1,0:T(8,128)S(1)} all-to-all(f32[16,32,128]{2,1,0:T(8,128)S(1)} %get-tuple-element.47), channel_id=1, replica_groups=mesh['prow'=16,'pcol'=16] {'pcol'}, dimensions={0} | all-to-all | bytes 524288 | tf_op jit(solution)/shard_map/all_to_all | solution.py:254
  61.8 0.0 collective-permute-done.2.other_ref
  61.8 1.5 %shard_map.61 = f32[2,32,2,64]{3,2,1,0:T(2,128)} custom-call(f32[16,32,128]{2,1,0:T(8,128)S(1)} %all_to_all.25.gathered_ref, bf16[4096,128]{1,0:T(8,128)(2,1)S(1)} %shard_map.60.mat_ref, f32[16,64,128]{2,1,0:T(8,128)S(1)} %collective-permute-done.2.other_ref, f32[2,32,128]{2,1,0:T(8,128)S(1)} %get-tuple-element.49.own_ref), custom_call_target="tpu_custom_call" | custom-call | tf_op jit(solution)/shard_map/pallas_call | solution.py:236
  (1 shorter events, 0.0 us)
Async XLA Ops:
  0.0 6.1 %copy-start = (f32[2,32,2,64]{3,2,1,0:T(2,128)S(1)}, f32[2,32,2,64]{3,2,1,0:T(2,128)}, u32[]{:S(2)}) copy-start(f32[2,32,2,64]{3,2,1,0:T(2,128)} %rhs_ref.1) | copy-start | bytes 98308
  0.0 9.5 %copy-start.1 = (f32[2,2,64,1024]{3,2,1,0:T(8,128)S(1)}, f32[2,2,64,1024]{3,2,1,0:T(8,128)}, u32[]{:S(2)}) copy-start(f32[2,2,64,1024]{3,2,1,0:T(8,128)} %param.12) | copy-start | bytes 3145732
  0.0 9.5 %copy-start.2 = (f32[2,64,1024]{2,1,0:T(8,128)S(1)}, f32[2,64,1024]{2,1,0:T(8,128)}, u32[]{:S(2)}) copy-start(f32[2,64,1024]{2,1,0:T(8,128)} %param.13) | copy-start | bytes 1572868
  6.2 4.9 %collective-permute-start = (f32[8,64,256]{2,1,0:T(8,128)S(1)}, f32[8,64,256]{2,1,0:T(8,128)S(1)}, u32[]{:S(2)}, u32[]{:S(2)}) collective-permute-start(f32[8,64,256]{2,1,0:T(8,128)S(1)} %shard_map.57.mine_ref), channel_id=1, source_target_pairs={{0,16},{16,0},{32,48},{48,32},{64,80},{80,64},{96,112},{112,96},{1... | collective-permute-start | bytes 1572872 | tf_op jit(solution)/shard_map/ppermute | solution.py:259
  48.9 1.7 %collective-permute-start.1 = (f32[2,32,128]{2,1,0:T(8,128)S(1)}, f32[2,32,128]{2,1,0:T(8,128)S(1)}, u32[]{:S(2)}, u32[]{:S(2)}) collective-permute-start(f32[2,32,128]{2,1,0:T(8,128)S(1)} %get-tuple-element.45), channel_id=1, source_target_pairs={{0,16},{16,0},{32,48},{48,32},{64,80},{80,64},{96,112},{112,96},{1... | collective-permute-start | bytes 98312 | tf_op jit(solution)/shard_map/ppermute | solution.py:280
  50.7 11.2 %collective-permute-start.2 = (f32[16,64,128]{2,1,0:T(8,128)S(1)}, f32[16,64,128]{2,1,0:T(8,128)S(1)}, u32[]{:S(2)}, u32[]{:S(2)}) collective-permute-start(f32[16,64,128]{2,1,0:T(8,128)S(1)} %get-tuple-element.48), channel_id=1, source_target_pairs={{0,16},{16,0},{32,48},{48,32},{64,80},{80,64},{96,112},{112,96},{1... | collective-permute-start | bytes 1572872 | tf_op jit(solution)/shard_map/ppermute | solution.py:285

commit v3 on v2

--- a/solution.py
+++ b/solution.py
@@ -1,3 +1,5 @@
+import functools
+
 import jax
 import jax.numpy as jnp
 from jax import lax
@@ -7,7 +9,7 @@
 
 BF = jnp.bfloat16
 F32 = jnp.float32
-CHUNKS = 4
+PLAN = ((2, 256), (3, 512))
 VMEM_LIMIT = 16 * 1024 * 1024
 UPDATE_VMEM = 53 * 1024 * 1024
 VMEM = pl.BlockSpec(memory_space=pltpu.VMEM)
@@ -29,24 +31,29 @@
     )
 
 
-def update_kernel(x_hbm, l_hbm, out_ref, x_buf, l_buf, total, sems):
-    chunk = x_buf.shape[3]
-
-    def copies(step):
-        lanes = pl.ds(pl.multiple_of(step * chunk, chunk), chunk)
+def update_kernel(x_hbm, l_hbm, out_ref, *scratch):
+    groups = len(PLAN)
+    x_bufs, l_bufs, (total, sems) = scratch[:groups], scratch[groups : 2 * groups], scratch[2 * groups :]
+
+    def copies(group, step):
+        count, width = PLAN[group]
+        first = sum(other for other, _ in PLAN[:group])
+        start = sum(other * wide for other, wide in PLAN[:group])
+        lanes = pl.ds(pl.multiple_of(start + step * width, 128), width)
         return (
-            pltpu.make_async_copy(l_hbm.at[:, :, :, lanes], l_buf.at[step], sems.at[step, 0]),
-            pltpu.make_async_copy(x_hbm.at[:, :, lanes], x_buf.at[step], sems.at[step, 1]),
+            pltpu.make_async_copy(l_hbm.at[:, :, :, lanes], l_bufs[group].at[step], sems.at[first + step, 0]),
+            pltpu.make_async_copy(x_hbm.at[:, :, lanes], x_bufs[group].at[step], sems.at[first + step, 1]),
         )
 
-    def begin(step, carry):
-        for copy in copies(step):
+    def begin(group, step, carry):
+        for copy in copies(group, step):
             copy.start()
         return carry
 
-    def multiply(step, carry):
-        for copy in copies(step):
+    def multiply(group, step, carry):
+        for copy in copies(group, step):
             copy.wait()
+        x_buf, l_buf = x_bufs[group], l_bufs[group]
         left = jnp.concatenate([x_buf[step, 0], x_buf[step, 1]], axis=1)
         rows = []
         for panel in range(2):
@@ -56,9 +63,11 @@
         total[...] += dot_split(left, jnp.concatenate(rows, axis=0))
         return carry
 
-    lax.fori_loop(0, CHUNKS, begin, 0)
+    for group in range(groups):
+        lax.fori_loop(0, PLAN[group][0], functools.partial(begin, group), 0)
     total[...] = jnp.zeros_like(total)
-    lax.fori_loop(0, CHUNKS, multiply, 0)
+    for group in range(groups):
+        lax.fori_loop(0, PLAN[group][0], functools.partial(multiply, group), 0)
     for level in range(out_ref.shape[0]):
         out_ref[level] = total[level * out_ref.shape[1] : (level + 1) * out_ref.shape[1], :]
 
@@ -66,17 +75,16 @@
 def update(x_done, l_below, rows):
     _, sides, depth = x_done.shape
     width = l_below.shape[2]
-    chunk = depth // CHUNKS
     return pl.pallas_call(
         update_kernel,
         in_specs=[pl.BlockSpec(memory_space=pltpu.HBM)] * 2,
         out_specs=VMEM,
         out_shape=jax.ShapeDtypeStruct((sides // rows, rows, 4 * width), F32),
         scratch_shapes=[
-            pltpu.VMEM((CHUNKS, 2, sides, chunk), F32),
-            pltpu.VMEM((CHUNKS, 2, 2, width, chunk), F32),
+            *(pltpu.VMEM((count, 2, sides, chunk), F32) for count, chunk in PLAN),
+            *(pltpu.VMEM((count, 2, 2, width, chunk), F32) for count, chunk in PLAN),
             pltpu.VMEM((sides, 4 * width), F32),
-            pltpu.SemaphoreType.DMA((CHUNKS, 2)),
+            pltpu.SemaphoreType.DMA((sum(count for count, _ in PLAN), 2)),
         ],
         compiler_params=pltpu.CompilerParams(vmem_limit_bytes=UPDATE_VMEM),
         cost_estimate=pl.CostEstimate(

time: 63.5 us -> 63.3 us (level)
  no operation moved by 1% of the time
where the time goes in v3:
time: 63.3 us; the launch traced here: 63.1 us
  blocking collectives  47.4 us (75%)
  Pallas kernels  9.61 us (15%)
  starting transfers between devices  4.59 us (7%)
  waiting for transfers between devices  1.4 us (2%)
    all_to_all x2, blocking collectives, per_device(): over_columns = lambda value: lax.all_to_all(value, 'pcol', 0, 0)  29 us
    all_to_all x1, blocking collectives, per_device(): lax.all_to_all(value, 'prow', 0, 0, axis_index_groups=same_core)  18.4 us
    pallas_call x1, Pallas kernels, update(): pl.pallas_call(update_kernel, in_specs=[pl.BlockSpec(memory_space=pltpu.H...  5.88 us
    pallas_call x8, Pallas kernels, call(): pl.pallas_call(kernel, in_specs=[VMEM] * len(args), out_specs=jax.tree.ma...  3.73 us
    ppermute x1, starting transfers between devices, per_device(): received = lax.ppermute(total, 'prow', swap)  3.31 us
  transfers between devices with their start and end apart: 3, of which 2 were waited for; matrix products, arithmetic and copies ran while one was open for 0% of the time, Pallas kernels for 2%

profile of v3, /device:TPU:1, one launch (start us, length us, event | category | flops | bytes accessed | tf_op | source)
XLA Modules:
  0.0 63.1 jit_solution(2186998592359447713)
XLA Ops:
  0.0 0.0 copy-start
  0.0 0.0 copy-start.1
  0.0 0.0 copy-start.2
  0.0 5.9 %shard_map.56.total_ref = f32[8,64,256]{2,1,0:T(8,128)S(1)} custom-call(f32[2,512,2048]{2,1,0:T(8,128)} %x_hbm.1, f32[2,2,64,2048]{3,2,1,0:T(8,128)} %l_hbm.1), custom_call_target="tpu_custom_call" | custom-call | flops 3221225472 | bytes 10485760 | tf_op jit(solution)/shard_map/pallas_call | solution.py:78
  5.9 0.0 copy-done
  5.9 0.1 shard_map.57.mine_ref
  6.0 3.3 %collective-permute-start = (f32[8,64,256]{2,1,0:T(8,128)S(1)}, f32[8,64,256]{2,1,0:T(8,128)S(1)}, u32[]{:S(2)}, u32[]{:S(2)}) collective-permute-start(f32[8,64,256]{2,1,0:T(8,128)S(1)} %shard_map.57.mine_ref), channel_id=1, source_target_pairs={{0,16},{16,0},{32,48},{48,32},{64,80},{80,64},{96,112},{112,96},{1... | collective-permute-start | bytes 1572872 | tf_op jit(solution)/shard_map/ppermute | solution.py:267
  9.3 0.0 copy-done.1
  9.3 0.0 copy-done.2
  9.3 0.5 conditional.2
  9.3 0.5 branch_1_fun.3
  9.8 1.0 %collective-permute-done.other_ref = f32[8,64,256]{2,1,0:T(8,128)S(1)} collective-permute-done((f32[8,64,256]{2,1,0:T(8,128)S(1)}, f32[8,64,256]{2,1,0:T(8,128)S(1)}, u32[]{:S(2)}, u32[]{:S(2)}) %collective-permute-start) | collective-permute-done | bytes 524320 | tf_op jit(solution)/shard_map/ppermute | solution.py:267
  10.8 0.1 shard_map.58
  10.9 37.8 %conditional.3 = ((f32[2,32,128]{2,1,0:T(8,128)S(1)}, f32[2,32,128]{2,1,0:T(8,128)S(1)}, f32[16,64,128]{2,1,0:T(8,128)S(1)})) conditional(s32[]{:T(128)} %convert_element_type.4, (f32[2,2,64,1024]{3,2,1,0:T(8,128)S(1)}, f32[16,128,128]{2,1,0:T(8,128)S(1)}) %tuple.29, (f32[8,64,256]{2,1,0:T(8,128)S(1)}, f32[16,128,128]{2,1,0:T(8,128)S(1)}, ...), branch_computations={%region_2.3_spmd, %region_3.4_spmd} | conditional | bytes 3145736 | solution.py:287
  10.9 18.4 %all_to_all.23.parts_ref = f32[8,64,256]{2,1,0:T(8,128)S(1)} all-to-all(f32[8,64,256]{2,1,0:T(8,128)S(1)} %get-tuple-element.35), channel_id=1, replica_groups={{0,32,64,96,128,160,192,224},{16,48,80,112,144,176,208,240},{1,33,65,97..., dimensions={0} | all-to-all | bytes 1048576 | tf_op jit(solution)/shard_map/cond/branch_1_fun/all_to_all | solution.py:263
  29.3 0.1 branch_1_fun.4
  29.4 18.3 %all_to_all.24.gathered_ref = f32[16,64,256]{2,1,0:T(8,128)S(1)} all-to-all(f32[16,64,256]{2,1,0:T(8,128)S(1)} %branch_1_fun.4), channel_id=1, replica_groups=mesh['prow'=16,'pcol'=16] {'pcol'}, dimensions={0} | all-to-all | bytes 2097152 | tf_op jit(solution)/shard_map/cond/branch_1_fun/all_to_all | solution.py:262
  47.7 1.0 %branch_1_fun.5 = (f32[2,32,128]{2,1,0:T(8,128)S(1)}, f32[2,32,128]{2,1,0:T(8,128)S(1)}, f32[16,64,128]{2,1,0:T(8,128)S(1)}) custom-call(f32[16,64,256]{2,1,0:T(8,128)S(1)} %all_to_all.24.gathered_ref, f32[16,128,128]{2,1,0:T(8,128)S(1)} %get-tuple-element.36.ready_ref, f32[2,2,64,1024]{3,2,1,0:T(8,128)S(1)} %get-tuple-element.37.inv_ref), custom_call_target="tpu_custom_call" | custom-call | tf_op jit(solution)/shard_map/cond/branch_1_fun/pallas_call | solution.py:244
  48.7 0.8 %collective-permute-start.1 = (f32[2,32,128]{2,1,0:T(8,128)S(1)}, f32[2,32,128]{2,1,0:T(8,128)S(1)}, u32[]{:S(2)}, u32[]{:S(2)}) collective-permute-start(f32[2,32,128]{2,1,0:T(8,128)S(1)} %get-tuple-element.45), channel_id=1, source_target_pairs={{0,16},{16,0},{32,48},{48,32},{64,80},{80,64},{96,112},{112,96},{1... | collective-permute-start | bytes 98312 | tf_op jit(solution)/shard_map/ppermute | solution.py:288
  49.6 0.5 shard_map.60.mat_ref
  50.1 0.4 collective-permute-done.1.other_ref
  50.5 0.4 collective-permute-start.2
  50.9 10.7 %all_to_all.25.gathered_ref = f32[16,32,128]{2,1,0:T(8,128)S(1)} all-to-all(f32[16,32,128]{2,1,0:T(8,128)S(1)} %get-tuple-element.47), channel_id=1, replica_groups=mesh['prow'=16,'pcol'=16] {'pcol'}, dimensions={0} | all-to-all | bytes 524288 | tf_op jit(solution)/shard_map/all_to_all | solution.py:262
  61.6 0.0 collective-permute-done.2.other_ref
  61.6 1.5 %shard_map.61 = f32[2,32,2,64]{3,2,1,0:T(2,128)} custom-call(f32[16,32,128]{2,1,0:T(8,128)S(1)} %all_to_all.25.gathered_ref, bf16[4096,128]{1,0:T(8,128)(2,1)S(1)} %shard_map.60.mat_ref, f32[16,64,128]{2,1,0:T(8,128)S(1)} %collective-permute-done.2.other_ref, f32[2,32,128]{2,1,0:T(8,128)S(1)} %get-tuple-element.49.own_ref), custom_call_target="tpu_custom_call" | custom-call | tf_op jit(solution)/shard_map/pallas_call | solution.py:244
  (1 shorter events, 0.0 us)
Async XLA Ops:
  0.0 5.9 %copy-start = (f32[2,32,2,64]{3,2,1,0:T(2,128)S(1)}, f32[2,32,2,64]{3,2,1,0:T(2,128)}, u32[]{:S(2)}) copy-start(f32[2,32,2,64]{3,2,1,0:T(2,128)} %rhs_ref.1) | copy-start | bytes 98308
  0.0 9.3 %copy-start.1 = (f32[2,2,64,1024]{3,2,1,0:T(8,128)S(1)}, f32[2,2,64,1024]{3,2,1,0:T(8,128)}, u32[]{:S(2)}) copy-start(f32[2,2,64,1024]{3,2,1,0:T(8,128)} %param.12) | copy-start | bytes 3145732
  0.0 9.3 %copy-start.2 = (f32[2,64,1024]{2,1,0:T(8,128)S(1)}, f32[2,64,1024]{2,1,0:T(8,128)}, u32[]{:S(2)}) copy-start(f32[2,64,1024]{2,1,0:T(8,128)} %param.13) | copy-start | bytes 1572868
  6.0 4.8 %collective-permute-start = (f32[8,64,256]{2,1,0:T(8,128)S(1)}, f32[8,64,256]{2,1,0:T(8,128)S(1)}, u32[]{:S(2)}, u32[]{:S(2)}) collective-permute-start(f32[8,64,256]{2,1,0:T(8,128)S(1)} %shard_map.57.mine_ref), channel_id=1, source_target_pairs={{0,16},{16,0},{32,48},{48,32},{64,80},{80,64},{96,112},{112,96},{1... | collective-permute-start | bytes 1572872 | tf_op jit(solution)/shard_map/ppermute | solution.py:267
  48.7 1.7 %collective-permute-start.1 = (f32[2,32,128]{2,1,0:T(8,128)S(1)}, f32[2,32,128]{2,1,0:T(8,128)S(1)}, u32[]{:S(2)}, u32[]{:S(2)}) collective-permute-start(f32[2,32,128]{2,1,0:T(8,128)S(1)} %get-tuple-element.45), channel_id=1, source_target_pairs={{0,16},{16,0},{32,48},{48,32},{64,80},{80,64},{96,112},{112,96},{1... | collective-permute-start | bytes 98312 | tf_op jit(solution)/shard_map/ppermute | solution.py:288
  50.5 11.2 %collective-permute-start.2 = (f32[16,64,128]{2,1,0:T(8,128)S(1)}, f32[16,64,128]{2,1,0:T(8,128)S(1)}, u32[]{:S(2)}, u32[]{:S(2)}) collective-permute-start(f32[16,64,128]{2,1,0:T(8,128)S(1)} %get-tuple-element.48), channel_id=1, source_target_pairs={{0,16},{16,0},{32,48},{48,32},{64,80},{80,64},{96,112},{112,96},{1... | collective-permute-start | bytes 1572872 | tf_op jit(solution)/shard_map/ppermute | solution.py:293

commit v4 on v3

--- a/solution.py
+++ b/solution.py
@@ -31,9 +31,9 @@
     )
 
 
-def update_kernel(x_hbm, l_hbm, out_ref, *scratch):
+def update_kernel(x_hbm, l_hbm, total, *scratch):
     groups = len(PLAN)
-    x_bufs, l_bufs, (total, sems) = scratch[:groups], scratch[groups : 2 * groups], scratch[2 * groups :]
+    x_bufs, l_bufs, sems = scratch[:groups], scratch[groups : 2 * groups], scratch[2 * groups]
 
     def copies(group, step):
         count, width = PLAN[group]
@@ -68,8 +68,6 @@
     total[...] = jnp.zeros_like(total)
     for group in range(groups):
         lax.fori_loop(0, PLAN[group][0], functools.partial(multiply, group), 0)
-    for level in range(out_ref.shape[0]):
-        out_ref[level] = total[level * out_ref.shape[1] : (level + 1) * out_ref.shape[1], :]
 
 
 def update(x_done, l_below, rows):
@@ -79,18 +77,17 @@
         update_kernel,
         in_specs=[pl.BlockSpec(memory_space=pltpu.HBM)] * 2,
         out_specs=VMEM,
-        out_shape=jax.ShapeDtypeStruct((sides // rows, rows, 4 * width), F32),
+        out_shape=jax.ShapeDtypeStruct((sides, 4 * width), F32),
         scratch_shapes=[
             *(pltpu.VMEM((count, 2, sides, chunk), F32) for count, chunk in PLAN),
             *(pltpu.VMEM((count, 2, 2, width, chunk), F32) for count, chunk in PLAN),
-            pltpu.VMEM((sides, 4 * width), F32),
             pltpu.SemaphoreType.DMA((sum(count for count, _ in PLAN), 2)),
         ],
         compiler_params=pltpu.CompilerParams(vmem_limit_bytes=UPDATE_VMEM),
         cost_estimate=pl.CostEstimate(
             flops=2 * 3 * sides * 2 * depth * 4 * width, bytes_accessed=x_done.size * 4 + l_below.size * 4, transcendentals=0
         ),
-    )(x_done, l_below)
+    )(x_done, l_below).reshape(sides // rows, rows, 4 * width)
 
 
 def subtract_kernel(rhs_ref, total_ref, out_ref):
@@ -114,25 +111,27 @@
     spread(spread_ref, -total)
 
 
-def weave(real, imag):
-    blocks = real.shape[1] // 128
-    low = lax.broadcasted_iota(jnp.int32, (real.shape[0], 128), 1) < 64
-    to_real, to_imag = [], []
-    for block in range(blocks):
-        lanes = slice(128 * block, 128 * (block + 1))
-        re, im = real[:, lanes], imag[:, lanes]
-        re_turned, im_turned = pltpu.roll(re, 64, 1), pltpu.roll(im, 64, 1)
-        to_real += [jnp.where(low, re, -im_turned), jnp.where(low, re_turned, -im)]
-        to_imag += [jnp.where(low, im, re_turned), jnp.where(low, im_turned, re)]
-    return jnp.concatenate([jnp.concatenate(to_real, axis=1), jnp.concatenate(to_imag, axis=1)], axis=0)
+def low_lanes(rows):
+    return lax.broadcasted_iota(jnp.int32, (rows, 128), 1) < 64
+
+
+def by_part(gathered_ref, lanes):
+    low = low_lanes(gathered_ref.shape[1])
+    real, imag = [], []
+    for pair in range(gathered_ref.shape[0] // 2):
+        first, second = gathered_ref[2 * pair, :, lanes], gathered_ref[2 * pair + 1, :, lanes]
+        real.append(jnp.where(low, first, pltpu.roll(second, 64, 1)))
+        imag.append(jnp.where(low, pltpu.roll(first, 64, 1), second))
+    return jnp.concatenate([jnp.concatenate(real, axis=1), jnp.concatenate(imag, axis=1)], axis=0)
 
 
 def apply_mat(gathered_ref, lanes, mat_high, mat_low):
-    blocks = [gathered_ref[block, :, lanes] for block in range(gathered_ref.shape[0])]
-    high, low = split(jnp.concatenate(blocks, axis=1))
+    high, low = split(by_part(gathered_ref, lanes))
     rows = high.shape[0]
     both = jnp.dot(jnp.concatenate([high, low], axis=0), mat_high, preferred_element_type=F32)
-    return both[:rows] + both[rows:] + jnp.dot(high, mat_low, preferred_element_type=F32)
+    terms = both[:rows] + both[rows:] + jnp.dot(high, mat_low, preferred_element_type=F32)
+    turned = pltpu.roll(terms[rows // 2 :], 64, 1)
+    return terms[: rows // 2] + jnp.where(low_lanes(rows // 2), -turned, turned)
 
 
 def masked(inv_ref, panel):
@@ -151,24 +150,25 @@
     out_ref[0] = jnp.zeros(out_ref.shape[1:], F32)
 
 
-def woven(real, imag):
-    return split(weave(real, imag).T)
+def turned_mat(real, imag):
+    return jnp.concatenate([real, imag], axis=0).T
 
 
 def ready_kernel(inv_ref, after_ref, out_ref):
     del after_ref
-    mat = weave(*masked(inv_ref, 1)).T
-    count = mat.shape[0] // out_ref.shape[0]
-    for block in range(out_ref.shape[0]):
-        out_ref[block] = mat[block * count : (block + 1) * count]
-
-
-def one_kernel(gathered_ref, ready_ref, inv_ref, ship_ref, held_ref, blank_ref):
+    blocks, count = out_ref.shape[0] // 2, out_ref.shape[1]
+    for panel in range(2):
+        mat = turned_mat(*masked(inv_ref, panel))
+        for block in range(blocks):
+            out_ref[panel * blocks + block] = mat[block * count : (block + 1) * count]
+
+
+def one_kernel(gathered_ref, ready_ref, ship_ref, held_ref, blank_ref):
     blank(blank_ref)
-    half, rows = gathered_ref.shape[2] // 2, held_ref.shape[1]
-    ready = jnp.concatenate([ready_ref[block] for block in range(ready_ref.shape[0])], axis=0)
-    for panel, mats in enumerate((woven(*masked(inv_ref, 0)), split(ready))):
-        applied = apply_mat(gathered_ref, slice(panel * half, (panel + 1) * half), *mats)
+    half, rows, blocks = gathered_ref.shape[2] // 2, held_ref.shape[1], ready_ref.shape[0] // 2
+    for panel in range(2):
+        mat = jnp.concatenate([ready_ref[panel * blocks + block] for block in range(blocks)], axis=0)
+        applied = apply_mat(gathered_ref, slice(panel * half, (panel + 1) * half), *split(mat))
         ship_ref[panel], held_ref[panel] = applied[:rows], applied[rows:]
 
 
@@ -213,10 +213,10 @@
     levels = product_ref.shape[0] // 2
     real = jnp.concatenate([product_ref[2 * level] for level in range(levels)], axis=1)
     imag = jnp.concatenate([product_ref[2 * level + 1] for level in range(levels)], axis=1)
-    return woven(real, imag)
-
-
-def weave_kernel(product_ref, mat_ref):
+    return split(turned_mat(real, imag))
+
+
+def turn_kernel(product_ref, mat_ref):
     depth = mat_ref.shape[0] // 2
     mat_ref[:depth, :], mat_ref[depth:, :] = product_mats(product_ref)
 
@@ -275,8 +275,9 @@
     whole = array(columns, rows, 2 * width)
 
     def solve(summed, inv_diag, ready):
+        del inv_diag
         reduced = call(reduce_kernel, array(columns, rows, 4 * width), over_levels(summed))
-        return tuple(call(one_kernel, [own, own, whole], over_columns(reduced), ready, inv_diag))
+        return tuple(call(one_kernel, [own, own, whole], over_columns(reduced), ready))
 
     def multiply(summed, inv_diag, gathered):
         del summed
@@ -286,8 +287,8 @@
 
     ship, held, product = lax.cond(upper, solve, multiply, summed, inv_diag, gathered)
     shipped = lax.ppermute(ship, "prow", swap)
-    mat = jax.ShapeDtypeStruct((4 * columns * width, 2 * width), BF)
-    mat = call(weave_kernel, mat, product)
+    mat = jax.ShapeDtypeStruct((2 * columns * width, 2 * width), BF)
+    mat = call(turn_kernel, mat, product)
     one = array(columns, rows // 2, 2 * width)
     held, one, product = call(spread_kernel, [own, one, whole], held, shipped, product, aliases={2: 2})
     other = lax.ppermute(product, "prow", swap)

time: 63.3 us -> 63.1 us (level)
  Pallas kernels: 9.61 us -> 8.69 us
    pallas_call x8, Pallas kernels: 3.73 us -> 2.84 us  [call(): pl.pallas_call(kernel, in_specs=[VMEM] * len(args), out_specs=jax.tree.ma...]
  transfers between devices with their start and end apart: 3 -> 3, of which waited for: 2 -> 2; matrix products, arithmetic and copies ran while one was open for 0% -> 0% of each run, Pallas kernels for 2% -> 1%
where the time goes in v4:
time: 63.1 us; the launch traced here: 62.9 us
  blocking collectives  47.4 us (75%)
  Pallas kernels  8.69 us (14%)
  starting transfers between devices  4.87 us (8%)
  waiting for transfers between devices  1.84 us (3%)
    all_to_all x2, blocking collectives, per_device(): over_columns = lambda value: lax.all_to_all(value, 'pcol', 0, 0)  29 us
    all_to_all x1, blocking collectives, per_device(): lax.all_to_all(value, 'prow', 0, 0, axis_index_groups=same_core)  18.4 us
    pallas_call x1, Pallas kernels, update(): pl.pallas_call(update_kernel, in_specs=[pl.BlockSpec(memory_space=pltpu.H...  5.85 us
    ppermute x1, starting transfers between devices, per_device(): received = lax.ppermute(total, 'prow', swap)  3.31 us
    pallas_call x8, Pallas kernels, call(): pl.pallas_call(kernel, in_specs=[VMEM] * len(args), out_specs=jax.tree.ma...  2.84 us
  transfers between devices with their start and end apart: 3, of which 2 were waited for; matrix products, arithmetic and copies ran while one was open for 0% of the time, Pallas kernels for 1%

profile of v4, /device:TPU:1, one launch (start us, length us, event | category | flops | bytes accessed | tf_op | source)
XLA Modules:
  0.0 62.9 jit_solution(14694527752608215862)
XLA Ops:
  0.0 0.0 copy-start
  0.0 0.0 copy-start.1
  0.0 0.0 copy-start.2
  0.0 5.9 %shard_map.56 = f32[512,256]{1,0:T(8,128)S(1)} custom-call(f32[2,512,2048]{2,1,0:T(8,128)} %x_hbm.1, f32[2,2,64,2048]{3,2,1,0:T(8,128)} %l_hbm.1), custom_call_target="tpu_custom_call" | custom-call | flops 3221225472 | bytes 10485760 | tf_op jit(solution)/shard_map/pallas_call | solution.py:76
  5.9 0.0 copy-done
  5.9 0.1 shard_map.57.mine_ref
  6.0 3.3 %collective-permute-start = (f32[8,64,256]{2,1,0:T(8,128)S(1)}, f32[8,64,256]{2,1,0:T(8,128)S(1)}, u32[]{:S(2)}, u32[]{:S(2)}) collective-permute-start(f32[8,64,256]{2,1,0:T(8,128)S(1)} %shard_map.57.mine_ref), channel_id=1, source_target_pairs={{0,16},{16,0},{32,48},{48,32},{64,80},{80,64},{96,112},{112,96},{1... | collective-permute-start | bytes 1572872 | tf_op jit(solution)/shard_map/ppermute | solution.py:267
  9.3 0.0 copy-done.1
  9.3 0.0 copy-done.2
  9.3 0.3 conditional.2
  9.3 0.3 branch_1_fun.3
  9.6 1.2 %collective-permute-done.other_ref = f32[8,64,256]{2,1,0:T(8,128)S(1)} collective-permute-done((f32[8,64,256]{2,1,0:T(8,128)S(1)}, f32[8,64,256]{2,1,0:T(8,128)S(1)}, u32[]{:S(2)}, u32[]{:S(2)}) %collective-permute-start) | collective-permute-done | bytes 524320 | tf_op jit(solution)/shard_map/ppermute | solution.py:267
  10.8 0.1 shard_map.58
  10.9 37.5 %conditional.3 = ((f32[2,32,128]{2,1,0:T(8,128)S(1)}, f32[2,32,128]{2,1,0:T(8,128)S(1)}, f32[16,64,128]{2,1,0:T(8,128)S(1)})) conditional(s32[]{:T(128)} %convert_element_type.4, (f32[2,2,64,1024]{3,2,1,0:T(8,128)S(1)}, f32[16,128,128]{2,1,0:T(8,128)S(1)}) %tuple.30, (f32[8,64,256]{2,1,0:T(8,128)S(1)}, f32[16,128,128]{2,1,0:T(8,128)S(1)}) %tuple.21), branch_computations={%region_2.3_spmd, %region_3.4_spmd} | conditional | bytes 3145736 | solution.py:288
  10.9 18.4 %all_to_all.23.parts_ref = f32[8,64,256]{2,1,0:T(8,128)S(1)} all-to-all(f32[8,64,256]{2,1,0:T(8,128)S(1)} %get-tuple-element.33), channel_id=1, replica_groups={{0,32,64,96,128,160,192,224},{16,48,80,112,144,176,208,240},{1,33,65,97..., dimensions={0} | all-to-all | bytes 1048576 | tf_op jit(solution)/shard_map/cond/branch_1_fun/all_to_all | solution.py:263
  29.3 0.1 branch_1_fun.4
  29.4 18.3 %all_to_all.24.gathered_ref = f32[16,64,256]{2,1,0:T(8,128)S(1)} all-to-all(f32[16,64,256]{2,1,0:T(8,128)S(1)} %branch_1_fun.4), channel_id=1, replica_groups=mesh['prow'=16,'pcol'=16] {'pcol'}, dimensions={0} | all-to-all | bytes 2097152 | tf_op jit(solution)/shard_map/cond/branch_1_fun/all_to_all | solution.py:262
  47.7 0.7 %branch_1_fun.5 = (f32[2,32,128]{2,1,0:T(8,128)S(1)}, f32[2,32,128]{2,1,0:T(8,128)S(1)}, f32[16,64,128]{2,1,0:T(8,128)S(1)}) custom-call(f32[16,64,256]{2,1,0:T(8,128)S(1)} %all_to_all.24.gathered_ref, f32[16,128,128]{2,1,0:T(8,128)S(1)} %get-tuple-element.34.ready_ref), custom_call_target="tpu_custom_call" | custom-call | tf_op jit(solution)/shard_map/cond/branch_1_fun/pallas_call | solution.py:244
  48.4 1.1 %collective-permute-start.1 = (f32[2,32,128]{2,1,0:T(8,128)S(1)}, f32[2,32,128]{2,1,0:T(8,128)S(1)}, u32[]{:S(2)}, u32[]{:S(2)}) collective-permute-start(f32[2,32,128]{2,1,0:T(8,128)S(1)} %get-tuple-element.42), channel_id=1, source_target_pairs={{0,16},{16,0},{32,48},{48,32},{64,80},{80,64},{96,112},{112,96},{1... | collective-permute-start | bytes 98312 | tf_op jit(solution)/shard_map/ppermute | solution.py:289
  49.6 0.2 shard_map.60.mat_ref
  49.8 0.7 %collective-permute-done.1.other_ref = f32[2,32,128]{2,1,0:T(8,128)S(1)} collective-permute-done((f32[2,32,128]{2,1,0:T(8,128)S(1)}, f32[2,32,128]{2,1,0:T(8,128)S(1)}, u32[]{:S(2)}, u32[]{:S(2)}) %collective-permute-start.1) | collective-permute-done | bytes 32800 | tf_op jit(solution)/shard_map/ppermute | solution.py:289
  50.4 0.4 collective-permute-start.2
  50.9 10.7 %all_to_all.25.gathered_ref = f32[16,32,128]{2,1,0:T(8,128)S(1)} all-to-all(f32[16,32,128]{2,1,0:T(8,128)S(1)} %get-tuple-element.44), channel_id=1, replica_groups=mesh['prow'=16,'pcol'=16] {'pcol'}, dimensions={0} | all-to-all | bytes 524288 | tf_op jit(solution)/shard_map/all_to_all | solution.py:262
  61.6 0.0 collective-permute-done.2.other_ref
  61.6 1.3 %shard_map.61 = f32[2,32,2,64]{3,2,1,0:T(2,128)} custom-call(f32[16,32,128]{2,1,0:T(8,128)S(1)} %all_to_all.25.gathered_ref, bf16[2048,128]{1,0:T(8,128)(2,1)S(1)} %shard_map.60.mat_ref, f32[16,64,128]{2,1,0:T(8,128)S(1)} %collective-permute-done.2.other_ref, f32[2,32,128]{2,1,0:T(8,128)S(1)} %get-tuple-element.46.own_ref), custom_call_target="tpu_custom_call" | custom-call | tf_op jit(solution)/shard_map/pallas_call | solution.py:244
  (1 shorter events, 0.0 us)
Async XLA Ops:
  0.0 5.9 %copy-start = (f32[2,32,2,64]{3,2,1,0:T(2,128)S(1)}, f32[2,32,2,64]{3,2,1,0:T(2,128)}, u32[]{:S(2)}) copy-start(f32[2,32,2,64]{3,2,1,0:T(2,128)} %rhs_ref.1) | copy-start | bytes 98308
  0.0 9.3 %copy-start.1 = (f32[2,2,64,1024]{3,2,1,0:T(8,128)S(1)}, f32[2,2,64,1024]{3,2,1,0:T(8,128)}, u32[]{:S(2)}) copy-start(f32[2,2,64,1024]{3,2,1,0:T(8,128)} %param.12) | copy-start | bytes 3145732
  0.0 9.3 %copy-start.2 = (f32[2,64,1024]{2,1,0:T(8,128)S(1)}, f32[2,64,1024]{2,1,0:T(8,128)}, u32[]{:S(2)}) copy-start(f32[2,64,1024]{2,1,0:T(8,128)} %param.13) | copy-start | bytes 1572868
  6.0 4.8 %collective-permute-start = (f32[8,64,256]{2,1,0:T(8,128)S(1)}, f32[8,64,256]{2,1,0:T(8,128)S(1)}, u32[]{:S(2)}, u32[]{:S(2)}) collective-permute-start(f32[8,64,256]{2,1,0:T(8,128)S(1)} %shard_map.57.mine_ref), channel_id=1, source_target_pairs={{0,16},{16,0},{32,48},{48,32},{64,80},{80,64},{96,112},{112,96},{1... | collective-permute-start | bytes 1572872 | tf_op jit(solution)/shard_map/ppermute | solution.py:267
  48.4 2.0 %collective-permute-start.1 = (f32[2,32,128]{2,1,0:T(8,128)S(1)}, f32[2,32,128]{2,1,0:T(8,128)S(1)}, u32[]{:S(2)}, u32[]{:S(2)}) collective-permute-start(f32[2,32,128]{2,1,0:T(8,128)S(1)} %get-tuple-element.42), channel_id=1, source_target_pairs={{0,16},{16,0},{32,48},{48,32},{64,80},{80,64},{96,112},{112,96},{1... | collective-permute-start | bytes 98312 | tf_op jit(solution)/shard_map/ppermute | solution.py:289
  50.4 11.2 %collective-permute-start.2 = (f32[16,64,128]{2,1,0:T(8,128)S(1)}, f32[16,64,128]{2,1,0:T(8,128)S(1)}, u32[]{:S(2)}, u32[]{:S(2)}) collective-permute-start(f32[16,64,128]{2,1,0:T(8,128)S(1)} %get-tuple-element.45), channel_id=1, source_target_pairs={{0,16},{16,0},{32,48},{48,32},{64,80},{80,64},{96,112},{112,96},{1... | collective-permute-start | bytes 1572872 | tf_op jit(solution)/shard_map/ppermute | solution.py:294

commit v5 on v4

--- a/solution.py
+++ b/solution.py
@@ -204,9 +204,10 @@
     both = jnp.dot(jnp.concatenate([left_high, left_low], axis=0), right_high, preferred_element_type=F32)
     product = both[: 2 * rows] + both[2 * rows :] + jnp.dot(left_high, right_low, preferred_element_type=F32)
     half = product.shape[1] // 2
+    real = product[:rows, :half] + product[rows:, half:]
+    imag = product[rows:, :half] - product[:rows, half:]
     for target in range(spread_ref.shape[0]):
-        spread_ref[target, 0] = product[:rows, :half] + product[rows:, half:]
-        spread_ref[target, 1] = product[rows:, :half] - product[:rows, half:]
+        spread_ref[target, 0], spread_ref[target, 1] = real, imag
 
 
 def product_mats(product_ref):

time: 63.1 us -> 63.1 us (level)
  no operation moved by 1% of the time
where the time goes in v5:
time: 63.1 us; the launch traced here: 62.9 us
  blocking collectives  47.4 us (75%)
  Pallas kernels  8.69 us (14%)
  starting transfers between devices  4.87 us (8%)
  waiting for transfers between devices  1.84 us (3%)
    all_to_all x2, blocking collectives, per_device(): over_columns = lambda value: lax.all_to_all(value, 'pcol', 0, 0)  29 us
    all_to_all x1, blocking collectives, per_device(): lax.all_to_all(value, 'prow', 0, 0, axis_index_groups=same_core)  18.4 us
    pallas_call x1, Pallas kernels, update(): pl.pallas_call(update_kernel, in_specs=[pl.BlockSpec(memory_space=pltpu.H...  5.85 us
    ppermute x1, starting transfers between devices, per_device(): received = lax.ppermute(total, 'prow', swap)  3.31 us
    pallas_call x8, Pallas kernels, call(): pl.pallas_call(kernel, in_specs=[VMEM] * len(args), out_specs=jax.tree.ma...  2.84 us
  transfers between devices with their start and end apart: 3, of which 2 were waited for; matrix products, arithmetic and copies ran while one was open for 0% of the time, Pallas kernels for 1%

profile of v5, /device:TPU:1, one launch (start us, length us, event | category | flops | bytes accessed | tf_op | source)
XLA Modules:
  0.0 62.9 jit_solution(14694527752608215862)
XLA Ops:
  0.0 0.0 copy-start
  0.0 0.0 copy-start.1
  0.0 0.0 copy-start.2
  0.0 5.9 %shard_map.56 = f32[512,256]{1,0:T(8,128)S(1)} custom-call(f32[2,512,2048]{2,1,0:T(8,128)} %x_hbm.1, f32[2,2,64,2048]{3,2,1,0:T(8,128)} %l_hbm.1), custom_call_target="tpu_custom_call" | custom-call | flops 3221225472 | bytes 10485760 | tf_op jit(solution)/shard_map/pallas_call | solution.py:76
  5.9 0.0 copy-done
  5.9 0.1 shard_map.57.mine_ref
  6.0 3.3 %collective-permute-start = (f32[8,64,256]{2,1,0:T(8,128)S(1)}, f32[8,64,256]{2,1,0:T(8,128)S(1)}, u32[]{:S(2)}, u32[]{:S(2)}) collective-permute-start(f32[8,64,256]{2,1,0:T(8,128)S(1)} %shard_map.57.mine_ref), channel_id=1, source_target_pairs={{0,16},{16,0},{32,48},{48,32},{64,80},{80,64},{96,112},{112,96},{1... | collective-permute-start | bytes 1572872 | tf_op jit(solution)/shard_map/ppermute | solution.py:268
  9.3 0.0 copy-done.1
  9.3 0.0 copy-done.2
  9.3 0.3 conditional.2
  9.3 0.3 branch_1_fun.3
  9.6 1.2 %collective-permute-done.other_ref = f32[8,64,256]{2,1,0:T(8,128)S(1)} collective-permute-done((f32[8,64,256]{2,1,0:T(8,128)S(1)}, f32[8,64,256]{2,1,0:T(8,128)S(1)}, u32[]{:S(2)}, u32[]{:S(2)}) %collective-permute-start) | collective-permute-done | bytes 524320 | tf_op jit(solution)/shard_map/ppermute | solution.py:268
  10.8 0.1 shard_map.58
  10.9 37.5 %conditional.3 = ((f32[2,32,128]{2,1,0:T(8,128)S(1)}, f32[2,32,128]{2,1,0:T(8,128)S(1)}, f32[16,64,128]{2,1,0:T(8,128)S(1)})) conditional(s32[]{:T(128)} %convert_element_type.4, (f32[2,2,64,1024]{3,2,1,0:T(8,128)S(1)}, f32[16,128,128]{2,1,0:T(8,128)S(1)}) %tuple.30, (f32[8,64,256]{2,1,0:T(8,128)S(1)}, f32[16,128,128]{2,1,0:T(8,128)S(1)}) %tuple.21), branch_computations={%region_2.3_spmd, %region_3.4_spmd} | conditional | bytes 3145736 | solution.py:289
  10.9 18.4 %all_to_all.23.parts_ref = f32[8,64,256]{2,1,0:T(8,128)S(1)} all-to-all(f32[8,64,256]{2,1,0:T(8,128)S(1)} %get-tuple-element.33), channel_id=1, replica_groups={{0,32,64,96,128,160,192,224},{16,48,80,112,144,176,208,240},{1,33,65,97..., dimensions={0} | all-to-all | bytes 1048576 | tf_op jit(solution)/shard_map/cond/branch_1_fun/all_to_all | solution.py:264
  29.3 0.1 branch_1_fun.4
  29.4 18.3 %all_to_all.24.gathered_ref = f32[16,64,256]{2,1,0:T(8,128)S(1)} all-to-all(f32[16,64,256]{2,1,0:T(8,128)S(1)} %branch_1_fun.4), channel_id=1, replica_groups=mesh['prow'=16,'pcol'=16] {'pcol'}, dimensions={0} | all-to-all | bytes 2097152 | tf_op jit(solution)/shard_map/cond/branch_1_fun/all_to_all | solution.py:263
  47.7 0.7 %branch_1_fun.5 = (f32[2,32,128]{2,1,0:T(8,128)S(1)}, f32[2,32,128]{2,1,0:T(8,128)S(1)}, f32[16,64,128]{2,1,0:T(8,128)S(1)}) custom-call(f32[16,64,256]{2,1,0:T(8,128)S(1)} %all_to_all.24.gathered_ref, f32[16,128,128]{2,1,0:T(8,128)S(1)} %get-tuple-element.34.ready_ref), custom_call_target="tpu_custom_call" | custom-call | tf_op jit(solution)/shard_map/cond/branch_1_fun/pallas_call | solution.py:245
  48.4 1.1 %collective-permute-start.1 = (f32[2,32,128]{2,1,0:T(8,128)S(1)}, f32[2,32,128]{2,1,0:T(8,128)S(1)}, u32[]{:S(2)}, u32[]{:S(2)}) collective-permute-start(f32[2,32,128]{2,1,0:T(8,128)S(1)} %get-tuple-element.42), channel_id=1, source_target_pairs={{0,16},{16,0},{32,48},{48,32},{64,80},{80,64},{96,112},{112,96},{1... | collective-permute-start | bytes 98312 | tf_op jit(solution)/shard_map/ppermute | solution.py:290
  49.6 0.2 shard_map.60.mat_ref
  49.8 0.7 %collective-permute-done.1.other_ref = f32[2,32,128]{2,1,0:T(8,128)S(1)} collective-permute-done((f32[2,32,128]{2,1,0:T(8,128)S(1)}, f32[2,32,128]{2,1,0:T(8,128)S(1)}, u32[]{:S(2)}, u32[]{:S(2)}) %collective-permute-start.1) | collective-permute-done | bytes 32800 | tf_op jit(solution)/shard_map/ppermute | solution.py:290
  50.4 0.4 collective-permute-start.2
  50.9 10.7 %all_to_all.25.gathered_ref = f32[16,32,128]{2,1,0:T(8,128)S(1)} all-to-all(f32[16,32,128]{2,1,0:T(8,128)S(1)} %get-tuple-element.44), channel_id=1, replica_groups=mesh['prow'=16,'pcol'=16] {'pcol'}, dimensions={0} | all-to-all | bytes 524288 | tf_op jit(solution)/shard_map/all_to_all | solution.py:263
  61.6 0.0 collective-permute-done.2.other_ref
  61.6 1.3 %shard_map.61 = f32[2,32,2,64]{3,2,1,0:T(2,128)} custom-call(f32[16,32,128]{2,1,0:T(8,128)S(1)} %all_to_all.25.gathered_ref, bf16[2048,128]{1,0:T(8,128)(2,1)S(1)} %shard_map.60.mat_ref, f32[16,64,128]{2,1,0:T(8,128)S(1)} %collective-permute-done.2.other_ref, f32[2,32,128]{2,1,0:T(8,128)S(1)} %get-tuple-element.46.own_ref), custom_call_target="tpu_custom_call" | custom-call | tf_op jit(solution)/shard_map/pallas_call | solution.py:245
  (1 shorter events, 0.0 us)
Async XLA Ops:
  0.0 5.9 %copy-start = (f32[2,32,2,64]{3,2,1,0:T(2,128)S(1)}, f32[2,32,2,64]{3,2,1,0:T(2,128)}, u32[]{:S(2)}) copy-start(f32[2,32,2,64]{3,2,1,0:T(2,128)} %rhs_ref.1) | copy-start | bytes 98308
  0.0 9.3 %copy-start.1 = (f32[2,2,64,1024]{3,2,1,0:T(8,128)S(1)}, f32[2,2,64,1024]{3,2,1,0:T(8,128)}, u32[]{:S(2)}) copy-start(f32[2,2,64,1024]{3,2,1,0:T(8,128)} %param.12) | copy-start | bytes 3145732
  0.0 9.3 %copy-start.2 = (f32[2,64,1024]{2,1,0:T(8,128)S(1)}, f32[2,64,1024]{2,1,0:T(8,128)}, u32[]{:S(2)}) copy-start(f32[2,64,1024]{2,1,0:T(8,128)} %param.13) | copy-start | bytes 1572868
  6.0 4.8 %collective-permute-start = (f32[8,64,256]{2,1,0:T(8,128)S(1)}, f32[8,64,256]{2,1,0:T(8,128)S(1)}, u32[]{:S(2)}, u32[]{:S(2)}) collective-permute-start(f32[8,64,256]{2,1,0:T(8,128)S(1)} %shard_map.57.mine_ref), channel_id=1, source_target_pairs={{0,16},{16,0},{32,48},{48,32},{64,80},{80,64},{96,112},{112,96},{1... | collective-permute-start | bytes 1572872 | tf_op jit(solution)/shard_map/ppermute | solution.py:268
  48.4 2.0 %collective-permute-start.1 = (f32[2,32,128]{2,1,0:T(8,128)S(1)}, f32[2,32,128]{2,1,0:T(8,128)S(1)}, u32[]{:S(2)}, u32[]{:S(2)}) collective-permute-start(f32[2,32,128]{2,1,0:T(8,128)S(1)} %get-tuple-element.42), channel_id=1, source_target_pairs={{0,16},{16,0},{32,48},{48,32},{64,80},{80,64},{96,112},{112,96},{1... | collective-permute-start | bytes 98312 | tf_op jit(solution)/shard_map/ppermute | solution.py:290
  50.4 11.2 %collective-permute-start.2 = (f32[16,64,128]{2,1,0:T(8,128)S(1)}, f32[16,64,128]{2,1,0:T(8,128)S(1)}, u32[]{:S(2)}, u32[]{:S(2)}) collective-permute-start(f32[16,64,128]{2,1,0:T(8,128)S(1)} %get-tuple-element.45), channel_id=1, source_target_pairs={{0,16},{16,0},{32,48},{48,32},{64,80},{80,64},{96,112},{112,96},{1... | collective-permute-start | bytes 1572872 | tf_op jit(solution)/shard_map/ppermute | solution.py:295
